TPU v7x, 256 devices: a whole 4x4x8 slice. The times are simulated.
256 devices in a mesh: dp: 16 (over y, x_lo, core), ctx: 16 (over x_hi, z).
Axes of the slice: x: 4 (x_hi: 2, x_lo: 2; x = x_hi * 2 + x_lo), y: 4, z: 8, core: 2. Of those that a mesh axis runs over, the one named last changes fastest.
Arguments:
- q_long: bfloat16 [16, 4096, 768], P('dp', 'ctx'), may hold values from -8 to 8
- k_long: bfloat16 [16, 4096, 128], P('dp', 'ctx'), may hold values from -8 to 8
- v_long: bfloat16 [16, 4096, 128], P('dp', 'ctx'), may hold values from -6 to 6
- o_long: bfloat16 [16, 4096, 768], P('dp', 'ctx'), may hold values from -4 to 4
- dout_long: bfloat16 [16, 4096, 768], P('dp', 'ctx'), may hold values from -6 to 6
- doc_lengths: int32 [16, 4], P('dp'), may hold values from 1 to 2048, 4096 in all within a row
- q_short: bfloat16 [16, 64, 128, 768], P('dp', 'ctx'), may hold values from -8 to 8
- k_short: bfloat16 [16, 64, 128, 128], P('dp', 'ctx'), may hold values from -8 to 8
- v_short: bfloat16 [16, 64, 128, 128], P('dp', 'ctx'), may hold values from -6 to 6
- o_short: bfloat16 [16, 64, 128, 768], P('dp', 'ctx'), may hold values from -4 to 4
- dout_short: bfloat16 [16, 64, 128, 768], P('dp', 'ctx'), may hold values from -6 to 6
- short_len: int32 [16, 64], P('dp', 'ctx'), may hold values from 1 to 128, as said below
- short_count: int32 [16, 16], P('dp', 'ctx'), may hold values from 0 to 4, as said below
Outputs:
- dq_long: bfloat16 [16, 4096, 768], P('dp', 'ctx')
- dk_long: bfloat16 [16, 4096, 128], P('dp', 'ctx')
- dv_long: bfloat16 [16, 4096, 128], P('dp', 'ctx')
- dq_short: bfloat16 [16, 64, 128, 768], P('dp', 'ctx')
- dk_short: bfloat16 [16, 64, 128, 128], P('dp', 'ctx')
- dv_short: bfloat16 [16, 64, 128, 128], P('dp', 'ctx')
Inputs may be any that keep to these rules, and one draw needn't show every extreme that they name: `doc_lengths`: each row sums to 4096; its longest document has exactly 2048 tokens. `short_count`: for each index of the second dimension the counts over the first dimension sum to exactly 32, and some device holds 4 live slots. `short_len`: some live slot holds a document of 128 rows; lengths of slots that are not live are ignored.
All inputs are finite; a program needn't handle non-finite values.
Results may differ from a plain program's by a relative error of at most 0.0085.
Values may be sent and summed in bfloat16 or wider, within the bound.
A program may use at most 128 MiB of HBM per device.

v0:
```python
import math

import jax
import jax.numpy as jnp
from jax import lax
from jax.sharding import PartitionSpec as P

H = 6
DH = 128


big_negative = -1e30


def stored_positions(row_index, shard_rows, shard_count):
    half_rows = shard_rows // 2
    owner_shard = row_index // shard_rows
    within = row_index % shard_rows
    early_pos = owner_shard * half_rows + within
    late_pos = (2 * shard_count - 1 - owner_shard) * half_rows + within - half_rows
    return jnp.where(within < half_rows, early_pos, late_pos)


def documents_of(positions, lengths):
    doc_ends = jnp.cumsum(lengths)
    return jnp.sum((positions[:, None] >= doc_ends[None, :]).astype(jnp.int32), axis=1)


def short_grads(queries, key_rows, value_rows, outputs, grad_out, lengths):
    slot_total = queries.shape[0]
    slot_rows = queries.shape[1]
    score_scale = 1.0 / math.sqrt(DH)
    query_heads = queries.reshape(slot_total, slot_rows, H, DH)
    grad_heads = grad_out.reshape(slot_total, slot_rows, H, DH)
    out_heads = outputs.reshape(slot_total, slot_rows, H, DH)
    row_index = jnp.arange(slot_rows, dtype=jnp.int32)
    live_rows = row_index[None, :] < lengths[:, None]
    causal = (row_index[None, :] <= row_index[:, None])[None]
    visible_mask = (causal & live_rows[:, None, :] & live_rows[:, :, None])[:, None]
    scores = (
        jnp.einsum("bihd,bjd->bhij", query_heads, key_rows, preferred_element_type=jnp.float32)
        * score_scale
    )
    row_max = jnp.max(jnp.where(visible_mask, scores, big_negative), axis=3, keepdims=True)
    weights = jnp.where(visible_mask, jnp.exp(scores - row_max), 0.0)
    row_sum = jnp.sum(weights, axis=3, keepdims=True)
    row_sum = jnp.where(live_rows[:, None, :, None], row_sum, 1.0)
    probs = weights / row_sum
    probs_round = probs.astype(jnp.bfloat16)
    delta = jnp.transpose(
        jnp.sum(grad_heads.astype(jnp.float32) * out_heads.astype(jnp.float32), axis=3), (0, 2, 1)
    )[:, :, :, None]
    dprobs = jnp.einsum(
        "bihd,bjd->bhij", grad_heads, value_rows, preferred_element_type=jnp.float32
    )
    dscores = (probs * (dprobs - delta)).astype(jnp.bfloat16)
    query_grad = (
        jnp.einsum("bhij,bjd->bihd", dscores, key_rows, preferred_element_type=jnp.float32)
        * score_scale
    )
    key_grad = (
        jnp.einsum("bhij,bihd->bjd", dscores, query_heads, preferred_element_type=jnp.float32)
        * score_scale
    )
    value_grad = jnp.einsum(
        "bhij,bihd->bjd", probs_round, grad_heads, preferred_element_type=jnp.float32
    )
    return (
        query_grad.reshape(slot_total, slot_rows, H * DH).astype(jnp.bfloat16),
        key_grad.astype(jnp.bfloat16),
        value_grad.astype(jnp.bfloat16),
    )


def body(
    q_long,
    k_long,
    v_long,
    o_long,
    dout_long,
    doc_lengths,
    q_short,
    k_short,
    v_short,
    o_short,
    dout_short,
    short_len,
    short_count,
):
    ctx_devices = lax.axis_size("ctx")
    ctx_rank = lax.axis_index("ctx")
    tok_rows = q_long.shape[1]
    seq_rows = tok_rows * ctx_devices
    score_scale = 1.0 / math.sqrt(DH)
    queries = q_long[0].reshape(tok_rows, H, DH)
    grad_out = dout_long[0].reshape(tok_rows, H, DH)
    outputs = o_long[0].reshape(tok_rows, H, DH)
    key_rows = k_long[0]
    value_rows = v_long[0]
    lengths = doc_lengths[0]
    query_pos = stored_positions(
        ctx_rank * tok_rows + jnp.arange(tok_rows, dtype=jnp.int32), tok_rows, ctx_devices
    )
    query_docs = documents_of(query_pos, lengths)
    delta = jnp.transpose(
        jnp.sum(grad_out.astype(jnp.float32) * outputs.astype(jnp.float32), axis=2)
    )[:, :, None]

    def visible(first_row, piece_rows):
        key_pos = stored_positions(
            first_row + jnp.arange(piece_rows, dtype=jnp.int32), tok_rows, ctx_devices
        )
        key_docs = documents_of(key_pos, lengths)
        return (
            (query_docs[:, None] == key_docs[None, :]) & (key_pos[None, :] <= query_pos[:, None])
        )[None]

    def add_stats(carried, piece, first_row):
        row_max, row_sum = carried
        visible_mask = visible(first_row, piece.shape[0])
        scores = (
            jnp.einsum("ihd,jd->hij", queries, piece, preferred_element_type=jnp.float32)
            * score_scale
        )
        new_max = jnp.maximum(
            row_max, jnp.max(jnp.where(visible_mask, scores, big_negative), axis=2, keepdims=True)
        )
        row_sum = row_sum * jnp.exp(row_max - new_max) + jnp.sum(
            jnp.where(visible_mask, jnp.exp(scores - new_max), 0.0), axis=2, keepdims=True
        )
        return (new_max, row_sum)

    def grad_adder(row_max, row_sum):

        def add_grads(carried, pieces, first_row):
            query_grad, key_grad, value_grad = carried
            key_piece, value_piece = pieces
            piece_rows = key_piece.shape[0]
            visible_mask = visible(first_row, piece_rows)
            scores = (
                jnp.einsum("ihd,jd->hij", queries, key_piece, preferred_element_type=jnp.float32)
                * score_scale
            )
            probs = jnp.where(visible_mask, jnp.exp(scores - row_max), 0.0) / row_sum
            probs_round = probs.astype(jnp.bfloat16)
            dprobs = jnp.einsum(
                "ihd,jd->hij", grad_out, value_piece, preferred_element_type=jnp.float32
            )
            dscores = (probs * (dprobs - delta)).astype(jnp.bfloat16)
            query_grad = (
                query_grad
                + jnp.einsum("hij,jd->ihd", dscores, key_piece, preferred_element_type=jnp.float32)
                * score_scale
            )
            key_part = (
                jnp.einsum("hij,ihd->jd", dscores, queries, preferred_element_type=jnp.float32)
                * score_scale
            )
            value_part = jnp.einsum(
                "hij,ihd->jd", probs_round, grad_out, preferred_element_type=jnp.float32
            )
            key_grad = lax.dynamic_update_slice_in_dim(
                key_grad,
                lax.dynamic_slice_in_dim(key_grad, first_row, piece_rows, 0) + key_part,
                first_row,
                0,
            )
            value_grad = lax.dynamic_update_slice_in_dim(
                value_grad,
                lax.dynamic_slice_in_dim(value_grad, first_row, piece_rows, 0) + value_part,
                first_row,
                0,
            )
            return (query_grad, key_grad, value_grad)

        return add_grads

    stats_init = (
        jnp.full((H, tok_rows, 1), big_negative, jnp.float32),
        jnp.zeros((H, tok_rows, 1), jnp.float32),
    )
    grads_init = (
        jnp.zeros((tok_rows, H, DH), jnp.float32),
        jnp.zeros((seq_rows, DH), jnp.float32),
        jnp.zeros((seq_rows, DH), jnp.float32),
    )
    whole_keys, whole_values = (
        lax.all_gather(key_rows, "ctx", axis=0, tiled=True),
        lax.all_gather(value_rows, "ctx", axis=0, tiled=True),
    )
    key_block = min(seq_rows, 2 * tok_rows)
    block_total = seq_rows // key_block
    block_starts = jnp.arange(block_total, dtype=jnp.int32) * key_block
    key_blocks = whole_keys.reshape(block_total, key_block, DH)
    value_blocks = whole_values.reshape(block_total, key_block, DH)

    def stats_step(carried, block_item):
        return (add_stats(carried, block_item[0], block_item[1]), None)

    (row_max, row_sum), unused_stats = lax.scan(stats_step, stats_init, (key_blocks, block_starts))
    add_grads = grad_adder(row_max, row_sum)

    def grads_step(carried, block_item):
        return (add_grads(carried, (block_item[0], block_item[1]), block_item[2]), None)

    (query_grad, key_grad, value_grad), unused_grads = lax.scan(
        grads_step, grads_init, (key_blocks, value_blocks, block_starts)
    )
    key_total, value_total = (
        lax.psum_scatter(key_grad, "ctx", scatter_dimension=0, tiled=True),
        lax.psum_scatter(value_grad, "ctx", scatter_dimension=0, tiled=True),
    )
    dq_long = query_grad.reshape(1, tok_rows, H * DH).astype(jnp.bfloat16)
    dk_long = key_total.astype(jnp.bfloat16)[None]
    dv_long = value_total.astype(jnp.bfloat16)[None]
    slot_total = q_short.shape[1]
    slot_index = jnp.arange(slot_total, dtype=jnp.int32)
    live_slots = slot_index < short_count[0, 0]
    dq_slots, dk_slots, dv_slots = short_grads(
        q_short[0], k_short[0], v_short[0], o_short[0], dout_short[0], short_len[0]
    )
    dq_short = jnp.where(live_slots[:, None, None], dq_slots, jnp.zeros_like(dq_slots))[None]
    dk_short = jnp.where(live_slots[:, None, None], dk_slots, jnp.zeros_like(dk_slots))[None]
    dv_short = jnp.where(live_slots[:, None, None], dv_slots, jnp.zeros_like(dv_slots))[None]
    return (dq_long, dk_long, dv_long, dq_short, dk_short, dv_short)


def solution(mesh):
    placed = (
        P("dp", "ctx", None),
        P("dp", "ctx", None),
        P("dp", "ctx", None),
        P("dp", "ctx", None),
        P("dp", "ctx", None),
        P("dp", None),
        P("dp", "ctx", None, None),
        P("dp", "ctx", None, None),
        P("dp", "ctx", None, None),
        P("dp", "ctx", None, None),
        P("dp", "ctx", None, None),
        P("dp", "ctx"),
        P("dp", "ctx"),
    )
    return jax.shard_map(
        body,
        mesh=mesh,
        in_specs=placed,
        out_specs=(
            P("dp", "ctx", None),
            P("dp", "ctx", None),
            P("dp", "ctx", None),
            P("dp", "ctx", None, None),
            P("dp", "ctx", None, None),
            P("dp", "ctx", None, None),
        ),
        check_vma=False,
    )
```

profile of v0, /device:TPU:8, one launch (start us, length us, event | category | flops | bytes accessed | tf_op | source)
XLA Modules:
  0.0 718.9 jit_solution(16580690266358806744)
XLA Ops:
  15.0 77.3 %all-gather.5.cloned.1.call-done = bf16[1,4096,128]{2,1,0:T(8,128)(2,1)} async-done(((bf16[1,256,128]{2,1,0:T(8,128)(2,1)}), bf16[1,4096,128]{2,1,0:T(8,128)(2,1)}) %all-gather.5.cloned.1.call-update) | async-done | bytes 1048592 | tf_op jit(solution)/shard_map/all_gather | solution.py:188
  92.3 32.1 %while.32 = (s32[]{:T(128)}, f32[6,256,1]{1,0,2:T(8,128)S(1)}, f32[6,256,1]{1,0,2:T(8,128)S(1)}, s32[256]{0:T(256)S(1)}, s32[8]{0:T(128)S(1)}, /*index=5*/s32[1,...) while((s32[]{:T(128)}, f32[6,256,1]{1,0,2:T(8,128)S(1)}, ...), condition=%wide.region_7.8_spmd.clone, body=%wide.region_3.7_spmd.clone.sunk | while | flops 207259648 | bytes 7302312 | solution.py:200
  124.4 45.9 %all-gather.7.cloned.1.call-done = bf16[1,4096,128]{2,1,0:T(8,128)(2,1)} async-done(((bf16[1,256,128]{2,1,0:T(8,128)(2,1)}), bf16[1,4096,128]{2,1,0:T(8,128)(2,1)}) %all-gather.7.cloned.1.call-update) | async-done | bytes 1048592 | tf_op jit(solution)/shard_map/all_gather | solution.py:189
  173.3 130.7 %while.33 = (s32[]{:T(128)}, f32[256,6,128]{0,2,1:T(8,128)S(1)}, f32[4096,128]{1,0:T(8,128)}, f32[4096,128]{1,0:T(8,128)}, bf16[8,512,128]{2,1,0:T(8,128)(2,1)},...) while((s32[]{:T(128)}, f32[256,6,128]{0,2,1:T(8,128)S(1)}, ...), condition=%wide.region_11.12_spmd.clone, body=%wide.region_9.11_spmd.clone.sunk | while | flops 1014131200 | bytes 32726932 | solution.py:206
  183.4 1.9 dynamic_update_slice.16
  185.3 2.5 fusion.113
  187.8 1.9 dynamic_update_slice.17
  201.7 2.5 fusion.113
  204.2 1.9 dynamic_update_slice.17
  216.2 1.9 dynamic_update_slice.16
  218.0 2.5 fusion.113
  220.6 1.9 dynamic_update_slice.17
  234.4 2.5 fusion.113
  250.7 2.5 fusion.113
  253.3 1.9 dynamic_update_slice.17
  267.1 2.5 fusion.113
  269.6 1.9 dynamic_update_slice.17
  281.6 1.9 dynamic_update_slice.16
  283.5 2.5 fusion.113
  286.0 1.9 dynamic_update_slice.17
  299.8 2.5 fusion.113
  314.8 2.2 fusion.53
  319.9 185.0 %reduce-scatter.3.cloned.1.call-done = f32[256,128]{1,0:T(8,128)} async-done(((f32[4096,128]{1,0:T(8,128)}), f32[256,128]{1,0:T(8,128)}) %reduce-scatter.3.cloned.1.call-update) | async-done | bytes 131088 | tf_op jit(solution)/shard_map/reduce_scatter | solution.py:210
  506.5 204.3 %reduce-scatter.5.cloned.1.call-done = f32[256,128]{1,0:T(8,128)} async-done(((f32[4096,128]{1,0:T(8,128)}), f32[256,128]{1,0:T(8,128)}) %reduce-scatter.5.cloned.1.call-update) | async-done | bytes 131088 | tf_op jit(solution)/shard_map/reduce_scatter | solution.py:211
  (369 shorter events, 135.1 us)
Async XLA Ops:
  7.2 302.0 %copy-start = (bf16[1,4,128,128]{3,2,1,0:T(8,128)(2,1)S(1)}, bf16[1,4,128,128]{3,2,1,0:T(8,128)(2,1)}, u32[]{:S(2)}) copy-start(bf16[1,4,128,128]{3,2,1,0:T(8,128)(2,1)} %param.24) | copy-start | bytes 393220
  7.2 7.4 %copy-start.9 = (bf16[1,256,768]{2,1,0:T(8,128)(2,1)S(1)}, bf16[1,256,768]{2,1,0:T(8,128)(2,1)}, u32[]{:S(2)}) copy-start(bf16[1,256,768]{2,1,0:T(8,128)(2,1)} %param.20) | copy-start | bytes 1179652
  7.2 85.1 %all-gather.5.cloned.1.call-start = ((), (), s32[]{:S(2)}) async-start(), calls=%async_computation.4 | async-start | bytes 1114112 | tf_op jit(solution)/shard_map/all_gather | solution.py:188
  7.9 162.4 %all-gather.7.cloned.1.call-start = ((), (), s32[]{:S(2)}) async-start(), calls=%async_computation.5 | async-start | bytes 1114112 | tf_op jit(solution)/shard_map/all_gather | solution.py:189
  8.7 496.3 %reduce-scatter.3.cloned.1.call-start = ((), (), s32[]{:S(2)}) async-start(), calls=%async_computation.2 | async-start | bytes 2228224 | tf_op jit(solution)/shard_map/reduce_scatter | solution.py:210
  185.3 4.4 copy-start.11
  185.3 4.4 copy-start.13
  185.3 4.4 copy-start.15
  185.3 4.4 copy-start.19
  201.6 4.4 copy-start.11
  201.6 4.4 copy-start.13
  201.6 4.4 copy-start.15
  201.6 4.4 copy-start.19
  218.0 4.4 copy-start.13
  218.0 4.4 copy-start.15
  218.0 4.4 copy-start.19
  250.7 4.4 copy-start.15
  250.7 4.4 copy-start.19
  267.1 4.4 copy-start.19
  283.4 4.4 copy-start.11
  283.5 4.4 copy-start.13
  283.5 4.4 copy-start.15
  283.5 4.4 copy-start.19
  304.1 406.7 %reduce-scatter.5.cloned.1.call-start = ((), (), s32[]{:S(2)}) async-start(), calls=%async_computation.3 | async-start | bytes 2228224 | tf_op jit(solution)/shard_map/reduce_scatter | solution.py:211
  (63 other events, 205.9 us)
Sparse Core Ops, SparseCore 0:
  10.6 81.6 all-gather.4
  94.9 75.3 all-gather.6
  304.2 200.6 reduce-scatter.2
  508.7 202.0 reduce-scatter.4
where the time goes:
time: 721 us; the launch traced here: 719 us
  waiting for transfers between devices  514 us (71%)
  matrix products  90.3 us (13%)
  local copies, waits for them, and re-layouts  53.7 us (7%)
  other arithmetic  28.1 us (4%)
  loops' own time  17.4 us (2%)
  between operations  14.8 us (2%)
    reduce_scatter x1, waiting for transfers between devices, body(): lax.psum_scatter(value_grad, 'ctx', scatter_dimension=0, tiled=True)  204 us
    reduce_scatter x1, waiting for transfers between devices, body(): lax.psum_scatter(key_grad, 'ctx', scatter_dimension=0, tiled=True)  185 us
    all_gather x1, waiting for transfers between devices, body(): lax.all_gather(key_rows, 'ctx', axis=0, tiled=True)  77.3 us
    all_gather x1, waiting for transfers between devices, body(): lax.all_gather(value_rows, 'ctx', axis=0, tiled=True)  45.9 us
    dot_general x8, matrix products, add_grads(): jnp.einsum('hij,ihd->jd', probs_round, grad_out, preferred_element_type=j...  20.1 us
    another operation x1, loops' own time, body(): lax.scan(grads_step, grads_init, (key_blocks, value_blocks, block_starts))  16.9 us
    dynamic_update_slice x8, local copies, waits for them, and re-layouts, add_grads(): lax.dynamic_update_slice_in_dim(value_grad, lax.dynamic_slice_in_dim(valu...  14.8 us
    dynamic_update_slice x8, local copies, waits for them, and re-layouts, add_grads(): lax.dynamic_update_slice_in_dim(key_grad, lax.dynamic_slice_in_dim(key_gr...  14.7 us
  transfers between devices with their start and end apart: 4, of which 4 were waited for; matrix products, arithmetic and copies ran while one was open for 7% of the time, Pallas kernels for 0%

commit v1 on v0

v1 whole, which is shorter than its diff:
```python
import math

import jax
import jax.numpy as jnp
from jax import lax
from jax.experimental import pallas as pl
from jax.experimental.pallas import tpu as pltpu
from jax.sharding import PartitionSpec as P

H = 6
DH = 128
CH = 128
NZ = 8
NCTX = 16
NCHUNK = 32
NDOC = 4
SLOTS = 4
HC = H * DH
PAIRS = tuple(range(0, HC, 2 * DH))
SCALE = 1.0 / math.sqrt(DH)
SCALE2 = SCALE * math.log2(math.e)
NEG = -1e30
ROOT_STEP = 0
LAST_STEP = 4

HOPS_UP = {
    (0, 0, 0): (3, 3, 3, 4, 3, 2, 1, 0),
    (0, 0, 1): (0, 0, 0, 0, 0, 4, 4, 4),
    (0, 1, 0): (0, 0, 3, 4, 3, 2, 4, 4),
    (0, 1, 1): (4, 3, 4, 3, 4, 3, 4, 3),
    (1, 0, 0): (4, 4, 4, 4, 4, 4, 4, 4),
    (1, 0, 1): (0, 0, 0, 0, 0, 4, 4, 4),
    (1, 1, 0): (4, 3, 4, 3, 4, 3, 4, 3),
    (1, 1, 1): (0, 0, 0, 0, 0, 0, 0, 0),
}
HOPS_DOWN = {
    (0, 0, 0): (4, 4, 4, 0, 0, 0, 0, 0),
    (0, 0, 1): (0, 1, 2, 3, 4, 3, 3, 3),
    (0, 1, 0): (1, 3, 4, 0, 1, 3, 3, 3),
    (0, 1, 1): (3, 4, 3, 4, 3, 4, 3, 4),
    (1, 0, 0): (3, 3, 3, 3, 3, 3, 3, 3),
    (1, 0, 1): (0, 1, 2, 3, 4, 3, 3, 3),
    (1, 1, 0): (3, 4, 3, 4, 3, 4, 3, 4),
    (1, 1, 1): (0, 0, 0, 0, 0, 0, 0, 0),
}


def packed(hops):
    return sum(h << (3 * z) for z, h in enumerate(hops))


def nt(a, b):
    return lax.dot_general(a, b, (((1,), (1,)), ((), ())), preferred_element_type=jnp.float32)


def nn(a, b):
    return lax.dot_general(a, b, (((1,), (0,)), ((), ())), preferred_element_type=jnp.float32)


def heads(ref, col):
    return jnp.concatenate([ref[:, col : col + DH], ref[:, col + DH : col + 2 * DH]], axis=0)


def row_delta(grads, outs):
    prod = grads.astype(jnp.float32) * outs.astype(jnp.float32)
    high = prod.astype(jnp.bfloat16)
    low = (prod - high.astype(jnp.float32)).astype(jnp.bfloat16)
    ones = jnp.ones((16, DH), jnp.bfloat16)
    return (nt(ones, high) + nt(ones, low))[0:1]


def kernel(
    q_hbm, k_hbm, v_hbm, o_hbm, do_hbm, doc_ref,
    qs_hbm, ks_hbm, vs_hbm, os_hbm, dos_hbm, slen_ref, scount_ref,
    dq_hbm, dk_hbm, dv_hbm, dqs_hbm, dks_hbm, dvs_hbm,
    kv, q_v, o_v, do_v, scores, m_v, l_v, delta_v, lo_v, dqt, acc, own,
    snd, rcv, rcvx, qs_v, ks_v, vs_v, os_v, dos_v, dq_v, dkv_v, dqs_v, dks_v, dvs_v,
    in_sem, out_sem, ag_send, ag_recv, rs_send, rs_recv, rsx_recv,
):
    f32, bf16 = jnp.float32, jnp.bfloat16
    c = lax.axis_index("ctx")
    x = c // NZ
    z = c - x * NZ
    late_own = 2 * NCTX - 1 - c
    z_up = lax.rem(z + 1, NZ)
    z_down = lax.rem(z + NZ - 1, NZ)
    across = (1 - x) * NZ + z
    beside = (x * NZ + z_up, x * NZ + z_down)

    def hops(direction, foreign, late, z_root):
        table = (HOPS_UP, HOPS_DOWN)[direction]
        code = jnp.where(x == 1, packed(table[1, foreign, late]), packed(table[0, foreign, late]))
        return (code >> (3 * z_root)) & 7

    def hops_dynamic(direction, foreign, late, z_root):
        up = [[hops(0, f, l, z_root) for l in (0, 1)] for f in (0, 1)]
        down = [[hops(1, f, l, z_root) for l in (0, 1)] for f in (0, 1)]
        pick = lambda t: jnp.where(
            foreign == 1, jnp.where(late == 1, t[1][1], t[1][0]), jnp.where(late == 1, t[0][1], t[0][0])
        )
        return jnp.where(direction == 1, pick(down), pick(up))

    def chunk_of(foreign, late, z_root):
        owner = jnp.where(foreign == 1, 1 - x, x) * NZ + z_root
        return jnp.where(late == 1, 2 * NCTX - 1 - owner, owner)

    def early_needs(j):
        return j <= c

    def late_needs(j):
        return (j >= 15 - c) & (j <= late_own)

    def ag_copy(j, way, target):
        return pltpu.make_async_remote_copy(
            src_ref=kv.at[j], dst_ref=kv.at[j], send_sem=ag_send.at[j, way], recv_sem=ag_recv.at[j],
            device_id={"ctx": target}, device_id_type=pl.DeviceIdType.MESH,
        )

    def rs_copy(j, way, target):
        return pltpu.make_async_remote_copy(
            src_ref=snd.at[j], dst_ref=rcv.at[way, j], send_sem=rs_send.at[j], recv_sem=rs_recv.at[way, j],
            device_id={"ctx": target}, device_id_type=pl.DeviceIdType.MESH,
        )

    def rsx_copy(j, late):
        return pltpu.make_async_remote_copy(
            src_ref=snd.at[j], dst_ref=rcvx.at[late], send_sem=rs_send.at[j], recv_sem=rsx_recv.at[late],
            device_id={"ctx": across}, device_id_type=pl.DeviceIdType.MESH,
        )

    kv_loads = [
        pltpu.make_async_copy(src.at[0, pl.ds(half * CH, CH)], kv.at[j, which], in_sem.at[2 * which + half])
        for which, src in ((0, k_hbm), (1, v_hbm))
        for half, j in ((0, c), (1, late_own))
    ]
    long_loads = [
        pltpu.make_async_copy(src.at[0], dst, in_sem.at[4 + n])
        for n, (src, dst) in enumerate(((q_hbm, q_v), (do_hbm, do_v), (o_hbm, o_v)))
    ]
    short_loads = [
        pltpu.make_async_copy(src.at[0], dst, in_sem.at[7 + n])
        for n, (src, dst) in enumerate(
            ((qs_hbm, qs_v), (ks_hbm, ks_v), (vs_hbm, vs_v), (os_hbm, os_v), (dos_hbm, dos_v))
        )
    ]
    for copy in kv_loads + long_loads + short_loads:
        copy.start()

    barrier = pltpu.get_barrier_semaphore()
    for target in beside + (across,):
        pl.semaphore_signal(
            barrier, inc=1, device_id={"ctx": target}, device_id_type=pl.DeviceIdType.MESH
        )
    pl.semaphore_wait(barrier, 3)

    def crosses(late):
        return (x == 1) | (late == 0)

    def arrives(late):
        return (x == 0) | (late == 0)

    for copy in kv_loads:
        copy.wait()
    for late in (0, 1):
        j = chunk_of(0, late, z)

        @pl.when(crosses(late))
        def _():
            ag_copy(j, 2, across).start()

    for late in (0, 1):
        j = chunk_of(0, late, z)
        for way in (0, 1):

            @pl.when(hops(way, 0, late, z) >= 1)
            def _():
                ag_copy(j, way, beside[way]).start()

    for copy in long_loads:
        copy.wait()
    halves = [(pl.ds(half * CH, CH), own_chunk) for half, own_chunk in ((0, c), (1, late_own))]
    ends = []
    total = doc_ref[0, 0]
    for d in range(NDOC):
        ends.append(total)
        if d + 1 < NDOC:
            total = total + doc_ref[0, d + 1]
    lane = lax.rem(lax.broadcasted_iota(jnp.int32, (1, 2 * DH), 1), CH)
    sub = lax.broadcasted_iota(jnp.int32, (CH, 1), 0)
    for half, (rows, own_chunk) in enumerate(halves):
        pos = own_chunk * CH + lane
        first = jnp.zeros((1, 2 * DH), jnp.int32)
        for end in ends:
            first = jnp.maximum(first, jnp.where(pos >= end, end, 0))
        lo_v[half] = first
        for col in PAIRS:
            delta_v[half, :, col : col + 2 * DH] = row_delta(heads(do_v.at[rows], col), heads(o_v.at[rows], col))
        m_v[half] = jnp.full((1, HC), NEG, f32)
        l_v[half] = jnp.zeros((1, HC), f32)
        dqt[half] = jnp.zeros((DH, HC), f32)

    def slot_of(half, j):
        return j if half == 0 else NCTX + j - (15 - c)

    def score_tile(half, j):
        rows, own_chunk = halves[half]
        keys = kv[j, 0]
        key_pos = j * CH + sub
        visible = (key_pos >= lo_v[half]) & (key_pos <= own_chunk * CH + lane)
        slot = slot_of(half, j)
        for col in PAIRS:
            cols = slice(col, col + 2 * DH)
            s = nt(keys, heads(q_v.at[rows], col)) * SCALE2
            s = jnp.where(visible, s, NEG)
            scores[slot, :, cols] = s
            m_old = m_v[half, :, cols]
            m_new = jnp.maximum(m_old, jnp.max(s, axis=0, keepdims=True))
            l_v[half, :, cols] = l_v[half, :, cols] * jnp.exp2(m_old - m_new) + jnp.sum(
                jnp.exp2(s - m_new), axis=0, keepdims=True
            )
            m_v[half, :, cols] = m_new

    def score_item(j, has):
        @pl.when(has & early_needs(j))
        def _():
            score_tile(0, j)

        @pl.when(has & late_needs(j))
        def _():
            score_tile(1, j)

    def short_slot(slot):
        length = jnp.where(slot < scount_ref[0, 0], slen_ref[0, slot], 0)
        keys = ks_v[slot]
        values = vs_v[slot]
        visible = (sub <= lane) & (lane < length)
        dk = jnp.zeros((CH, DH), f32)
        dv = jnp.zeros((CH, DH), f32)
        for col in PAIRS:
            queries = heads(qs_v.at[slot], col)
            grads = heads(dos_v.at[slot], col)
            delta = row_delta(grads, heads(os_v.at[slot], col))
            s = jnp.where(visible, nt(keys, queries) * SCALE2, NEG)
            e = jnp.exp2(s - jnp.max(s, axis=0, keepdims=True))
            inverse = jnp.where(lane < length, 1.0 / jnp.sum(e, axis=0, keepdims=True), 0.0)
            p = e * inverse
            ds = (p * (nt(values, grads) - delta)).astype(bf16)
            dv = dv + nn(p.astype(bf16), grads)
            dk = dk + nn(ds, queries)
            dq = lax.dot_general(keys, ds, (((0,), (0,)), ((), ())), preferred_element_type=f32)
            for n in (0, 1):
                dqs_v[slot, :, col + n * DH : col + (n + 1) * DH] = (
                    dq[:, n * DH : (n + 1) * DH].T * SCALE
                ).astype(bf16)
        dks_v[slot] = (dk * SCALE).astype(bf16)
        dvs_v[slot] = dv.astype(bf16)

    score_item(c, c >= 0)
    score_item(late_own, c >= 0)

    for late in (0, 1):
        j = chunk_of(1, late, z)

        @pl.when(arrives(late))
        def _():
            ag_copy(j, 2, across).wait_recv()
            for way in (0, 1):

                @pl.when(hops(way, 1, late, z) >= 1)
                def _():
                    ag_copy(j, way, beside[way]).start()

    def foreign_score(late, carry):
        score_item(chunk_of(1, late, z), arrives(late))
        return carry

    lax.fori_loop(0, 2, foreign_score, 0)

    for copy in short_loads:
        copy.wait()

    def gather_step(step, carry):
        for foreign in (0, 1):
            for late in (0, 1):
                for way in (0, 1):
                    z_root = lax.rem(z + NZ + (step if way == 1 else -step), NZ)
                    j = chunk_of(foreign, late, z_root)
                    reach = hops(way, foreign, late, z_root)

                    @pl.when(reach >= step)
                    def _():
                        ag_copy(j, way, beside[way]).wait_recv()

                    @pl.when(reach >= step + 1)
                    def _():
                        ag_copy(j, way, beside[way]).start()

        short_slot(step - 1)

        def item(n, carry):
            foreign, late, way = n // 4, lax.rem(n // 2, 2), lax.rem(n, 2)
            z_root = lax.rem(z + NZ + jnp.where(way == 1, step, -step), NZ)
            score_item(chunk_of(foreign, late, z_root), hops_dynamic(way, foreign, late, z_root) >= step)
            return carry

        return lax.fori_loop(0, 8, item, carry)

    lax.fori_loop(1, LAST_STEP + 1, gather_step, 0)

    short_stores = [
        pltpu.make_async_copy(src, dst.at[0], out_sem.at[n])
        for n, (src, dst) in enumerate(((dqs_v, dqs_hbm), (dks_v, dks_hbm), (dvs_v, dvs_hbm)))
    ]
    for copy in short_stores:
        copy.start()

    for half in (0, 1):
        m_v[half] = m_v[half] + jnp.log2(l_v[half])

    def grad_tile(half, j):
        rows, own_chunk = halves[half]
        keys = kv[j, 0]
        values = kv[j, 1]
        slot = slot_of(half, j)
        dk = acc[0]
        dv = acc[1]
        for col in PAIRS:
            cols = slice(col, col + 2 * DH)
            queries = heads(q_v.at[rows], col)
            grads = heads(do_v.at[rows], col)
            p = jnp.exp2(scores[slot, :, cols] - m_v[half, :, cols])
            ds = (p * (nt(values, grads) - delta_v[half, :, cols])).astype(bf16)
            dv = dv + nn(p.astype(bf16), grads)
            dk = dk + nn(ds, queries)
            dqt[half, :, cols] += lax.dot_general(
                keys, ds, (((0,), (0,)), ((), ())), preferred_element_type=f32
            )
        acc[0] = dk
        acc[1] = dv

    def grad_item(j):
        acc[...] = jnp.zeros((2, CH, DH), f32)

        @pl.when(early_needs(j))
        def _():
            grad_tile(0, j)

        @pl.when(late_needs(j))
        def _():
            grad_tile(1, j)

    def scatter_step(back, carry):
        step = LAST_STEP - back

        def item(n, carry):
            foreign, late, way = n // 4, lax.rem(n // 2, 2), lax.rem(n, 2)
            z_root = lax.rem(z + NZ + jnp.where(way == 1, step, -step), NZ)
            j = chunk_of(foreign, late, z_root)
            reach = hops_dynamic(way, foreign, late, z_root)

            @pl.when(reach >= step)
            def _():
                grad_item(j)
                home = jnp.where(way == 1, beside[0], beside[1])
                copy = rs_copy(j, way, home)

                @pl.when(reach >= step + 1)
                def _():
                    copy.wait_recv()
                    acc[...] += rcv[way, j].astype(f32)

                snd[j] = acc[...].astype(bf16)
                copy.start()

            return carry

        return lax.fori_loop(0, 8, item, carry)

    lax.fori_loop(0, LAST_STEP, scatter_step, 0)

    def collect(foreign, late, j):
        for way in (0, 1):

            @pl.when(hops_dynamic(way, foreign, late, z) >= 1)
            def _():
                rs_copy(j, way, beside[way]).wait_recv()
                acc[...] += rcv[way, j].astype(f32)

    def foreign_root(late, carry):
        j = chunk_of(1, late, z)

        @pl.when(arrives(late))
        def _():
            grad_item(j)
            collect(1, late, j)
            snd[j] = acc[...].astype(bf16)
            rsx_copy(j, late).start()

        return carry

    lax.fori_loop(0, 2, foreign_root, 0)

    def own_root(late, carry):
        grad_item(chunk_of(0, late, z))
        own[late] = acc[...]
        return carry

    lax.fori_loop(0, 2, own_root, 0)

    for half, (rows, own_chunk) in enumerate(halves):
        for col in range(0, HC, DH):
            dq_v[rows, col : col + DH] = (dqt[half, :, col : col + DH].T * SCALE).astype(bf16)
    dq_store = pltpu.make_async_copy(dq_v, dq_hbm.at[0], out_sem.at[3])
    dq_store.start()

    def own_total(late, carry):
        acc[...] = own[late]
        j = chunk_of(0, late, z)
        collect(0, late, j)

        @pl.when(crosses(late))
        def _():
            rsx_copy(j, late).wait_recv()
            acc[...] += rcvx[late].astype(f32)

        rows = pl.ds(pl.multiple_of(late * CH, CH), CH)
        dkv_v[0, rows] = (acc[0] * SCALE).astype(bf16)
        dkv_v[1, rows] = acc[1].astype(bf16)
        return carry

    lax.fori_loop(0, 2, own_total, 0)
    kv_stores = [
        pltpu.make_async_copy(dkv_v.at[n], dst.at[0], out_sem.at[4 + n]) for n, dst in enumerate((dk_hbm, dv_hbm))
    ]
    for copy in kv_stores:
        copy.start()

    for late in (0, 1):
        j = chunk_of(0, late, z)

        @pl.when(crosses(late))
        def _():
            ag_copy(j, 2, across).wait_send()

        for foreign in (0, 1):
            j = chunk_of(foreign, late, z)
            for way in (0, 1):

                @pl.when(hops(way, foreign, late, z) >= 1)
                def _():
                    ag_copy(j, way, beside[way]).wait_send()

        @pl.when(arrives(late))
        def _():
            rsx_copy(chunk_of(1, late, z), late).wait_send()

    def sent_step(step, carry):
        def item(n, carry):
            foreign, late, way = n // 4, lax.rem(n // 2, 2), lax.rem(n, 2)
            z_root = lax.rem(z + NZ + jnp.where(way == 1, step, -step), NZ)
            j = chunk_of(foreign, late, z_root)
            reach = hops_dynamic(way, foreign, late, z_root)

            @pl.when(reach >= step)
            def _():
                rs_copy(j, way, beside[0]).wait_send()

            @pl.when(reach >= step + 1)
            def _():
                ag_copy(j, way, beside[0]).wait_send()

            return carry

        return lax.fori_loop(0, 8, item, carry)

    lax.fori_loop(1, LAST_STEP + 1, sent_step, 0)

    for copy in short_stores + [dq_store] + kv_stores:
        copy.wait()


def body(*args):
    bf16, f32 = jnp.bfloat16, jnp.float32
    tok = args[0].shape[1]
    any_spec = pl.BlockSpec(memory_space=pl.ANY)
    smem_spec = pl.BlockSpec(memory_space=pltpu.SMEM)
    in_specs = [any_spec] * 5 + [smem_spec] + [any_spec] * 5 + [smem_spec] * 2
    out_shape = [jax.ShapeDtypeStruct(args[n].shape, bf16) for n in (0, 1, 2, 6, 7, 8)]
    dma = pltpu.SemaphoreType.DMA
    scratch = [
        pltpu.VMEM((NCHUNK, 2, CH, DH), bf16),
        pltpu.VMEM((tok, HC), bf16),
        pltpu.VMEM((tok, HC), bf16),
        pltpu.VMEM((tok, HC), bf16),
        pltpu.VMEM((33, CH, HC), f32),
        pltpu.VMEM((2, 1, HC), f32),
        pltpu.VMEM((2, 1, HC), f32),
        pltpu.VMEM((2, 1, HC), f32),
        pltpu.VMEM((2, 1, 2 * DH), jnp.int32),
        pltpu.VMEM((2, DH, HC), f32),
        pltpu.VMEM((2, CH, DH), f32),
        pltpu.VMEM((2, 2, CH, DH), f32),
        pltpu.VMEM((NCHUNK, 2, CH, DH), bf16),
        pltpu.VMEM((2, NCHUNK, 2, CH, DH), bf16),
        pltpu.VMEM((2, 2, CH, DH), bf16),
        pltpu.VMEM((SLOTS, CH, HC), bf16),
        pltpu.VMEM((SLOTS, CH, DH), bf16),
        pltpu.VMEM((SLOTS, CH, DH), bf16),
        pltpu.VMEM((SLOTS, CH, HC), bf16),
        pltpu.VMEM((SLOTS, CH, HC), bf16),
        pltpu.VMEM((tok, HC), bf16),
        pltpu.VMEM((2, tok, DH), bf16),
        pltpu.VMEM((SLOTS, CH, HC), bf16),
        pltpu.VMEM((SLOTS, CH, DH), bf16),
        pltpu.VMEM((SLOTS, CH, DH), bf16),
        dma((12,)),
        dma((6,)),
        dma((NCHUNK, 3)),
        dma((NCHUNK,)),
        dma((NCHUNK,)),
        dma((2, NCHUNK)),
        dma((2,)),
    ]
    return tuple(
        pl.pallas_call(
            kernel,
            out_shape=out_shape,
            in_specs=in_specs,
            out_specs=[any_spec] * 6,
            scratch_shapes=scratch,
            compiler_params=pltpu.CompilerParams(
                collective_id=0, has_side_effects=True, vmem_limit_bytes=48 * 1024 * 1024
            ),
            name="attention_backward",
        )(*args)
    )


def solution(mesh):
    seq = P("dp", "ctx", None)
    slot = P("dp", "ctx", None, None)
    return jax.shard_map(
        body,
        mesh=mesh,
        in_specs=(seq,) * 5 + (P("dp", None),) + (slot,) * 5 + (P("dp", "ctx"),) * 2,
        out_specs=(seq, seq, seq, slot, slot, slot),
        check_vma=False,
    )
```

time: 721 us -> 80.9 us (0.11)
  waiting for transfers between devices: 514 us -> 0 us
  matrix products: 90.3 us -> 0 us
  Pallas kernels: 0 us -> 65 us
  local copies, waits for them, and re-layouts: 53.7 us -> 14.1 us
  other arithmetic: 28.1 us -> 0 us
  loops' own time: 17.4 us -> 0 us
  between operations: 14.8 us -> 1.36 us
    reduce_scatter x2 -> x0, waiting for transfers between devices: 389 us -> none  [the longest x1 204 us: body(): lax.psum_scatter(value_grad, 'ctx', scatter_dimension=0, tiled=True)]
    all_gather x2 -> x0, waiting for transfers between devices: 123 us -> none  [the longest x1 77.3 us: body(): lax.all_gather(key_rows, 'ctx', axis=0, tiled=True)]
    dot_general x53 -> x0, matrix products: 90.3 us -> none  [the longest x8 20.1 us: add_grads(): jnp.einsum('hij,ihd->jd', probs_round, grad_out, preferred_element_type=j...]
    pallas_call x0 -> x1, Pallas kernels: none -> 65 us  [body(): pl.pallas_call(kernel, out_shape=out_shape, in_specs=in_specs, out_specs=...]
    dynamic_update_slice x16 -> x0, local copies, waits for them, and re-layouts: 29.5 us -> none  [the longest x8 14.8 us: add_grads(): lax.dynamic_update_slice_in_dim(value_grad, lax.dynamic_slice_in_dim(valu...]
    another operation x2 -> x0, loops' own time: 17.4 us -> none  [the longest x1 16.9 us: body(): lax.scan(grads_step, grads_init, (key_blocks, value_blocks, block_starts))]
    select_n x35 -> x0, other arithmetic: 11.8 us -> none  [the longest x33 10.8 us: stored_positions(): return jnp.where(within < half_rows, early_pos, late_pos)]
    dynamic_slice x16 -> x0, local copies, waits for them, and re-layouts: 9.42 us -> none  [body(): lax.scan(stats_step, stats_init, (key_blocks, block_starts))]
  transfers between devices with their start and end apart: 4 -> 0, of which waited for: 4 -> 0; matrix products, arithmetic and copies ran while one was open for 7% -> 0% of each run, Pallas kernels for 0% -> 0%
where the time goes in v1:
time: 80.9 us; the launch traced here: 80.4 us
  Pallas kernels  65 us (80%)
  local copies, waits for them, and re-layouts  14.1 us (17%)
  between operations  1.36 us (2%)
    pallas_call x1, Pallas kernels, body(): pl.pallas_call(kernel, out_shape=out_shape, in_specs=in_specs, out_specs=...  65 us
    unnamed x30, local copies, waits for them, and re-layouts  14.1 us

profile of v1, /device:TPU:8, one launch (start us, length us, event | category | flops | bytes accessed | tf_op | source)
XLA Modules:
  0.0 80.4 jit_solution(5480730778751392991)
XLA Ops:
  0.6 0.0 copy-start.11
  0.6 0.0 copy-start.10
  1.3 0.0 copy-done.11
  1.3 0.0 copy-done.10
  1.3 0.0 copy-start
  1.4 1.1 %copy-done = bf16[1,4,128,768]{3,2,1,0:T(8,128)(2,1)S(1)} copy-done((bf16[1,4,128,768]{3,2,1,0:T(8,128)(2,1)S(1)}, bf16[1,4,128,768]{3,2,1,0:T(8,128)(2,1)}, u32[]{:S(2)}) %copy-start) | copy-done | bytes 786456
  2.5 0.0 copy-start.1
  2.5 1.1 %copy-done.1 = bf16[1,4,128,768]{3,2,1,0:T(8,128)(2,1)S(1)} copy-done((bf16[1,4,128,768]{3,2,1,0:T(8,128)(2,1)S(1)}, bf16[1,4,128,768]{3,2,1,0:T(8,128)(2,1)}, u32[]{:S(2)}) %copy-start.1) | copy-done | bytes 786456
  3.6 0.0 copy-start.2
  3.6 1.1 %copy-done.2 = bf16[1,4,128,768]{3,2,1,0:T(8,128)(2,1)S(1)} copy-done((bf16[1,4,128,768]{3,2,1,0:T(8,128)(2,1)S(1)}, bf16[1,4,128,768]{3,2,1,0:T(8,128)(2,1)}, u32[]{:S(2)}) %copy-start.2) | copy-done | bytes 786456
  4.7 1.0 %copy-done.3 = bf16[1,256,768]{2,1,0:T(8,128)(2,1)S(1)} copy-done((bf16[1,256,768]{2,1,0:T(8,128)(2,1)S(1)}, bf16[1,256,768]{2,1,0:T(8,128)(2,1)}, u32[]{:S(2)}) %copy-start.3) | copy-done | bytes 393240
  5.7 1.0 %copy-done.4 = bf16[1,256,768]{2,1,0:T(8,128)(2,1)S(1)} copy-done((bf16[1,256,768]{2,1,0:T(8,128)(2,1)S(1)}, bf16[1,256,768]{2,1,0:T(8,128)(2,1)}, u32[]{:S(2)}) %copy-start.4) | copy-done | bytes 393240
  6.7 1.0 %copy-done.5 = bf16[1,256,768]{2,1,0:T(8,128)(2,1)S(1)} copy-done((bf16[1,256,768]{2,1,0:T(8,128)(2,1)S(1)}, bf16[1,256,768]{2,1,0:T(8,128)(2,1)}, u32[]{:S(2)}) %copy-start.5) | copy-done | bytes 393240
  7.7 0.9 %copy-done.6 = bf16[1,4,128,128]{3,2,1,0:T(8,128)(2,1)S(1)} copy-done((bf16[1,4,128,128]{3,2,1,0:T(8,128)(2,1)S(1)}, bf16[1,4,128,128]{3,2,1,0:T(8,128)(2,1)}, u32[]{:S(2)}) %copy-start.6) | copy-done | bytes 131096
  8.6 0.9 %copy-done.7 = bf16[1,4,128,128]{3,2,1,0:T(8,128)(2,1)S(1)} copy-done((bf16[1,4,128,128]{3,2,1,0:T(8,128)(2,1)S(1)}, bf16[1,4,128,128]{3,2,1,0:T(8,128)(2,1)}, u32[]{:S(2)}) %copy-start.7) | copy-done | bytes 131096
  9.5 0.8 %copy-done.8 = bf16[1,256,128]{2,1,0:T(8,128)(2,1)S(1)} copy-done((bf16[1,256,128]{2,1,0:T(8,128)(2,1)S(1)}, bf16[1,256,128]{2,1,0:T(8,128)(2,1)}, u32[]{:S(2)}) %copy-start.8) | copy-done | bytes 65560
  10.4 0.8 %copy-done.9 = bf16[1,256,128]{2,1,0:T(8,128)(2,1)S(1)} copy-done((bf16[1,256,128]{2,1,0:T(8,128)(2,1)S(1)}, bf16[1,256,128]{2,1,0:T(8,128)(2,1)}, u32[]{:S(2)}) %copy-start.9) | copy-done | bytes 65560
  11.2 65.0 %attention_backward.1 = (bf16[1,256,768]{2,1,0:T(8,128)(2,1)S(1)}, bf16[1,256,128]{2,1,0:T(8,128)(2,1)S(1)}, bf16[1,256,128]{2,1,0:T(8,128)(2,1)S(1)}, bf16[1,4,...) custom-call(bf16[1,256,768]{2,1,0:T(8,128)(2,1)S(1)} %copy-done.3, ...), custom_call_target="tpu_custom_call" | custom-call | tf_op jit(solution)/shard_map/attention_backward/pallas_call | solution.py:525
  76.2 0.7 copy.26
  77.0 0.6 copy.27
  77.6 0.6 copy.28
  78.2 0.9 %copy.29 = bf16[1,4,128,768]{3,2,1,0:T(8,128)(2,1)} copy(bf16[1,4,128,768]{3,2,1,0:T(8,128)(2,1)S(1)} %get-tuple-element.15) | data formatting | bytes 1572864
  79.1 0.7 copy.30
  79.8 0.7 copy.31
  (7 shorter events, 0.0 us)
Async XLA Ops:
  0.6 0.7 copy-start.11
  0.6 0.7 copy-start.10
  1.3 1.1 %copy-start = (bf16[1,4,128,768]{3,2,1,0:T(8,128)(2,1)S(1)}, bf16[1,4,128,768]{3,2,1,0:T(8,128)(2,1)}, u32[]{:S(2)}) copy-start(bf16[1,4,128,768]{3,2,1,0:T(8,128)(2,1)} %qs_hbm.1) | copy-start | bytes 2359300
  2.5 1.1 %copy-start.1 = (bf16[1,4,128,768]{3,2,1,0:T(8,128)(2,1)S(1)}, bf16[1,4,128,768]{3,2,1,0:T(8,128)(2,1)}, u32[]{:S(2)}) copy-start(bf16[1,4,128,768]{3,2,1,0:T(8,128)(2,1)} %os_hbm.1) | copy-start | bytes 2359300
  3.6 1.1 %copy-start.2 = (bf16[1,4,128,768]{3,2,1,0:T(8,128)(2,1)S(1)}, bf16[1,4,128,768]{3,2,1,0:T(8,128)(2,1)}, u32[]{:S(2)}) copy-start(bf16[1,4,128,768]{3,2,1,0:T(8,128)(2,1)} %dos_hbm.1) | copy-start | bytes 2359300
  4.7 1.0 %copy-start.3 = (bf16[1,256,768]{2,1,0:T(8,128)(2,1)S(1)}, bf16[1,256,768]{2,1,0:T(8,128)(2,1)}, u32[]{:S(2)}) copy-start(bf16[1,256,768]{2,1,0:T(8,128)(2,1)} %q_hbm.1) | copy-start | bytes 1179652
  5.7 1.0 %copy-start.4 = (bf16[1,256,768]{2,1,0:T(8,128)(2,1)S(1)}, bf16[1,256,768]{2,1,0:T(8,128)(2,1)}, u32[]{:S(2)}) copy-start(bf16[1,256,768]{2,1,0:T(8,128)(2,1)} %o_hbm.1) | copy-start | bytes 1179652
  6.7 1.0 %copy-start.5 = (bf16[1,256,768]{2,1,0:T(8,128)(2,1)S(1)}, bf16[1,256,768]{2,1,0:T(8,128)(2,1)}, u32[]{:S(2)}) copy-start(bf16[1,256,768]{2,1,0:T(8,128)(2,1)} %do_hbm.1) | copy-start | bytes 1179652
  7.7 0.9 %copy-start.6 = (bf16[1,4,128,128]{3,2,1,0:T(8,128)(2,1)S(1)}, bf16[1,4,128,128]{3,2,1,0:T(8,128)(2,1)}, u32[]{:S(2)}) copy-start(bf16[1,4,128,128]{3,2,1,0:T(8,128)(2,1)} %ks_hbm.1) | copy-start | bytes 393220
  8.6 0.9 %copy-start.7 = (bf16[1,4,128,128]{3,2,1,0:T(8,128)(2,1)S(1)}, bf16[1,4,128,128]{3,2,1,0:T(8,128)(2,1)}, u32[]{:S(2)}) copy-start(bf16[1,4,128,128]{3,2,1,0:T(8,128)(2,1)} %vs_hbm.1) | copy-start | bytes 393220
  9.5 0.8 %copy-start.8 = (bf16[1,256,128]{2,1,0:T(8,128)(2,1)S(1)}, bf16[1,256,128]{2,1,0:T(8,128)(2,1)}, u32[]{:S(2)}) copy-start(bf16[1,256,128]{2,1,0:T(8,128)(2,1)} %k_hbm.1) | copy-start | bytes 196612
  10.4 0.8 %copy-start.9 = (bf16[1,256,128]{2,1,0:T(8,128)(2,1)S(1)}, bf16[1,256,128]{2,1,0:T(8,128)(2,1)}, u32[]{:S(2)}) copy-start(bf16[1,256,128]{2,1,0:T(8,128)(2,1)} %v_hbm.1) | copy-start | bytes 196612

commit v2 on v1

--- a/solution.py
+++ b/solution.py
@@ -73,7 +73,7 @@
     q_hbm, k_hbm, v_hbm, o_hbm, do_hbm, doc_ref,
     qs_hbm, ks_hbm, vs_hbm, os_hbm, dos_hbm, slen_ref, scount_ref,
     dq_hbm, dk_hbm, dv_hbm, dqs_hbm, dks_hbm, dvs_hbm,
-    kv, q_v, o_v, do_v, scores, m_v, l_v, delta_v, lo_v, dqt, acc, own,
+    kv, q_v, o_v, do_v, scores, ds_v, m_v, l_v, lse_v, delta_v, lo_v, dqt, acc, own,
     snd, rcv, rcvx, qs_v, ks_v, vs_v, os_v, dos_v, dq_v, dkv_v, dqs_v, dks_v, dvs_v,
     in_sem, out_sem, ag_send, ag_recv, rs_send, rs_recv, rsx_recv,
 ):
@@ -87,18 +87,22 @@
     across = (1 - x) * NZ + z
     beside = (x * NZ + z_up, x * NZ + z_down)
 
+    codes = [
+        [
+            [jnp.where(x == 1, packed(table[1, foreign, late]), packed(table[0, foreign, late])) for late in (0, 1)]
+            for foreign in (0, 1)
+        ]
+        for table in (HOPS_UP, HOPS_DOWN)
+    ]
+
     def hops(direction, foreign, late, z_root):
-        table = (HOPS_UP, HOPS_DOWN)[direction]
-        code = jnp.where(x == 1, packed(table[1, foreign, late]), packed(table[0, foreign, late]))
+        code = codes[direction][foreign][late]
         return (code >> (3 * z_root)) & 7
 
     def hops_dynamic(direction, foreign, late, z_root):
-        up = [[hops(0, f, l, z_root) for l in (0, 1)] for f in (0, 1)]
-        down = [[hops(1, f, l, z_root) for l in (0, 1)] for f in (0, 1)]
-        pick = lambda t: jnp.where(
-            foreign == 1, jnp.where(late == 1, t[1][1], t[1][0]), jnp.where(late == 1, t[0][1], t[0][0])
-        )
-        return jnp.where(direction == 1, pick(down), pick(up))
+        by_way = [[jnp.where(direction == 1, codes[1][f][l], codes[0][f][l]) for l in (0, 1)] for f in (0, 1)]
+        by_late = [jnp.where(late == 1, both[1], both[0]) for both in by_way]
+        return (jnp.where(foreign == 1, by_late[1], by_late[0]) >> (3 * z_root)) & 7
 
     def chunk_of(foreign, late, z_root):
         owner = jnp.where(foreign == 1, 1 - x, x) * NZ + z_root
@@ -195,39 +199,43 @@
         lo_v[half] = first
         for col in PAIRS:
             delta_v[half, :, col : col + 2 * DH] = row_delta(heads(do_v.at[rows], col), heads(o_v.at[rows], col))
-        m_v[half] = jnp.full((1, HC), NEG, f32)
-        l_v[half] = jnp.zeros((1, HC), f32)
-        dqt[half] = jnp.zeros((DH, HC), f32)
+        m_v[half] = jnp.full((8, HC), NEG, f32)
+        l_v[half] = jnp.zeros((8, HC), f32)
+    dqt[0] = jnp.zeros((DH, HC), f32)
 
     def slot_of(half, j):
         return j if half == 0 else NCTX + j - (15 - c)
 
-    def score_tile(half, j):
-        rows, own_chunk = halves[half]
+    def score_tiles(which, j):
         keys = kv[j, 0]
         key_pos = j * CH + sub
-        visible = (key_pos >= lo_v[half]) & (key_pos <= own_chunk * CH + lane)
-        slot = slot_of(half, j)
-        for col in PAIRS:
-            cols = slice(col, col + 2 * DH)
-            s = nt(keys, heads(q_v.at[rows], col)) * SCALE2
-            s = jnp.where(visible, s, NEG)
-            scores[slot, :, cols] = s
-            m_old = m_v[half, :, cols]
-            m_new = jnp.maximum(m_old, jnp.max(s, axis=0, keepdims=True))
-            l_v[half, :, cols] = l_v[half, :, cols] * jnp.exp2(m_old - m_new) + jnp.sum(
-                jnp.exp2(s - m_new), axis=0, keepdims=True
-            )
-            m_v[half, :, cols] = m_new
+        for half in which:
+            rows, own_chunk = halves[half]
+            visible = (key_pos >= lo_v[half]) & (key_pos <= own_chunk * CH + lane)
+            bias = jnp.where(visible, 0.0, NEG)
+            slot = slot_of(half, j)
+            for col in PAIRS:
+                cols = slice(col, col + 2 * DH)
+                s = nt(keys, heads(q_v.at[rows], col)) * SCALE2 + bias
+                scores[slot, :, cols] = s
+                s = s.reshape(CH // 8, 8, 2 * DH)
+                m_old = m_v[half, :, cols]
+                m_new = jnp.maximum(m_old, jnp.max(s, axis=0))
+                m_v[half, :, cols] = m_new
+                l_v[half, :, cols] = l_v[half, :, cols] * jnp.exp2(m_old - m_new) + jnp.sum(
+                    jnp.exp2(s - m_new[None]), axis=0
+                )
+
+    def for_needed(j, has, tiles):
+        early, late = early_needs(j), late_needs(j)
+        for which, wanted in (((0, 1), early & late), ((0,), early & ~late), ((1,), late & ~early)):
+
+            @pl.when(has & wanted)
+            def _():
+                tiles(which, j)
 
     def score_item(j, has):
-        @pl.when(has & early_needs(j))
-        def _():
-            score_tile(0, j)
-
-        @pl.when(has & late_needs(j))
-        def _():
-            score_tile(1, j)
+        for_needed(j, has, score_tiles)
 
     def short_slot(slot):
         length = jnp.where(slot < scount_ref[0, 0], slen_ref[0, slot], 0)
@@ -315,39 +323,34 @@
         copy.start()
 
     for half in (0, 1):
-        m_v[half] = m_v[half] + jnp.log2(l_v[half])
-
-    def grad_tile(half, j):
-        rows, own_chunk = halves[half]
-        keys = kv[j, 0]
+        m = jnp.max(m_v[half], axis=0, keepdims=True)
+        lse_v[half] = m + jnp.log2(jnp.sum(l_v[half] * jnp.exp2(m_v[half] - m), axis=0, keepdims=True))
+
+    def grad_tiles(which, j):
         values = kv[j, 1]
-        slot = slot_of(half, j)
-        dk = acc[0]
-        dv = acc[1]
-        for col in PAIRS:
-            cols = slice(col, col + 2 * DH)
-            queries = heads(q_v.at[rows], col)
-            grads = heads(do_v.at[rows], col)
-            p = jnp.exp2(scores[slot, :, cols] - m_v[half, :, cols])
-            ds = (p * (nt(values, grads) - delta_v[half, :, cols])).astype(bf16)
-            dv = dv + nn(p.astype(bf16), grads)
-            dk = dk + nn(ds, queries)
-            dqt[half, :, cols] += lax.dot_general(
-                keys, ds, (((0,), (0,)), ((), ())), preferred_element_type=f32
-            )
-        acc[0] = dk
-        acc[1] = dv
+        p_parts, ds_parts, q_parts, do_parts = [], [], [], []
+        for half in which:
+            rows, own_chunk = halves[half]
+            slot = slot_of(half, j)
+            for col in PAIRS:
+                cols = slice(col, col + 2 * DH)
+                grads = heads(do_v.at[rows], col)
+                p = jnp.exp2(scores[slot, :, cols] - lse_v[half, :, cols])
+                ds = (p * (nt(values, grads) - delta_v[half, :, cols])).astype(bf16)
+                ds_v[slot, :, cols] = ds
+                p_parts.append(p.astype(bf16))
+                ds_parts.append(ds)
+                q_parts.append(heads(q_v.at[rows], col))
+                do_parts.append(grads)
+        acc[0] = nn(jnp.concatenate(ds_parts, axis=1), jnp.concatenate(q_parts, axis=0))
+        acc[1] = nn(jnp.concatenate(p_parts, axis=1), jnp.concatenate(do_parts, axis=0))
 
     def grad_item(j):
-        acc[...] = jnp.zeros((2, CH, DH), f32)
-
-        @pl.when(early_needs(j))
-        def _():
-            grad_tile(0, j)
-
-        @pl.when(late_needs(j))
-        def _():
-            grad_tile(1, j)
+        @pl.when(~(early_needs(j) | late_needs(j)))
+        def _():
+            acc[...] = jnp.zeros((2, CH, DH), f32)
+
+        for_needed(j, c >= 0, grad_tiles)
 
     def scatter_step(back, carry):
         step = LAST_STEP - back
@@ -407,6 +410,29 @@
 
     lax.fori_loop(0, 2, own_root, 0)
 
+    def tn(a, b):
+        return lax.dot_general(a, b, (((0,), (0,)), ((), ())), preferred_element_type=f32)
+
+    def dq_early(first, count):
+        keys = kv[pl.ds(first, count), 0].reshape(count * CH, DH)
+        for col in PAIRS:
+            cols = slice(col, col + 2 * DH)
+            dqt[0, :, cols] += tn(keys, ds_v[pl.ds(first, count), :, cols].reshape(count * CH, 2 * DH))
+
+    def dq_early_two(n, carry):
+        dq_early(2 * n, 2)
+        return carry
+
+    lax.fori_loop(0, (c + 1) // 2, dq_early_two, 0)
+
+    @pl.when(lax.rem(c, 2) == 0)
+    def _():
+        dq_early(c, 1)
+
+    keys = kv[pl.ds(15 - c, 17), 0].reshape(17 * CH, DH)
+    for col in PAIRS:
+        cols = slice(col, col + 2 * DH)
+        dqt[1, :, cols] = tn(keys, ds_v[NCTX : NCTX + 17, :, cols].reshape(17 * CH, 2 * DH))
     for half, (rows, own_chunk) in enumerate(halves):
         for col in range(0, HC, DH):
             dq_v[rows, col : col + DH] = (dqt[half, :, col : col + DH].T * SCALE).astype(bf16)
@@ -479,10 +505,19 @@
         copy.wait()
 
 
+def emit(*refs):
+    sem = refs[12]
+    copies = [pltpu.make_async_copy(refs[n], refs[6 + n], sem.at[n]) for n in range(6)]
+    for copy in copies:
+        copy.start()
+    for copy in copies:
+        copy.wait()
+
+
 def body(*args):
     bf16, f32 = jnp.bfloat16, jnp.float32
     tok = args[0].shape[1]
-    any_spec = pl.BlockSpec(memory_space=pl.ANY)
+    any_spec = pl.BlockSpec(memory_space=pltpu.HBM)
     smem_spec = pl.BlockSpec(memory_space=pltpu.SMEM)
     in_specs = [any_spec] * 5 + [smem_spec] + [any_spec] * 5 + [smem_spec] * 2
     out_shape = [jax.ShapeDtypeStruct(args[n].shape, bf16) for n in (0, 1, 2, 6, 7, 8)]
@@ -493,7 +528,9 @@
         pltpu.VMEM((tok, HC), bf16),
         pltpu.VMEM((tok, HC), bf16),
         pltpu.VMEM((33, CH, HC), f32),
-        pltpu.VMEM((2, 1, HC), f32),
+        pltpu.VMEM((33, CH, HC), bf16),
+        pltpu.VMEM((2, 8, HC), f32),
+        pltpu.VMEM((2, 8, HC), f32),
         pltpu.VMEM((2, 1, HC), f32),
         pltpu.VMEM((2, 1, HC), f32),
         pltpu.VMEM((2, 1, 2 * DH), jnp.int32),
@@ -521,18 +558,27 @@
         dma((2, NCHUNK)),
         dma((2,)),
     ]
+    grads = pl.pallas_call(
+        kernel,
+        out_shape=out_shape,
+        in_specs=in_specs,
+        out_specs=[any_spec] * 6,
+        scratch_shapes=scratch,
+        compiler_params=pltpu.CompilerParams(
+            collective_id=0, has_side_effects=True, vmem_limit_bytes=60 * 1024 * 1024
+        ),
+        name="attention_backward",
+    )(*args)
     return tuple(
         pl.pallas_call(
-            kernel,
+            emit,
             out_shape=out_shape,
-            in_specs=in_specs,
+            in_specs=[any_spec] * 6,
             out_specs=[any_spec] * 6,
-            scratch_shapes=scratch,
-            compiler_params=pltpu.CompilerParams(
-                collective_id=0, has_side_effects=True, vmem_limit_bytes=48 * 1024 * 1024
-            ),
-            name="attention_backward",
-        )(*args)
+            scratch_shapes=[dma((6,))],
+            compiler_params=pltpu.CompilerParams(vmem_limit_bytes=60 * 1024 * 1024),
+            name="emit",
+        )(*grads)
     )
 
 

time: 80.9 us -> 109 us (1.35)
  Pallas kernels: 65 us -> 106 us
  local copies, waits for them, and re-layouts: 14.1 us -> 0 us
    pallas_call x0 -> x1, Pallas kernels: none -> 48.8 us  [body(): pl.pallas_call(emit, out_shape=out_shape, in_specs=[any_spec] * 6, out_sp...]
    unnamed x30 -> x0, local copies, waits for them, and re-layouts: 14.1 us -> none
    pallas_call x1, Pallas kernels: 65 us -> 57.6 us  [body(): pl.pallas_call(kernel, out_shape=out_shape, in_specs=in_specs, out_specs=...]
where the time goes in v2:
time: 109 us; the launch traced here: 108 us
  Pallas kernels  106 us (97%)
  between operations  1.29 us (1%)
    pallas_call x1, Pallas kernels, body(): pl.pallas_call(kernel, out_shape=out_shape, in_specs=in_specs, out_specs=...  57.6 us
    pallas_call x1, Pallas kernels, body(): pl.pallas_call(emit, out_shape=out_shape, in_specs=[any_spec] * 6, out_sp...  48.8 us

profile of v2, /device:TPU:8, one launch (start us, length us, event | category | flops | bytes accessed | tf_op | source)
XLA Modules:
  0.0 107.7 jit_solution(10351442394288391660)
XLA Ops:
  1.3 57.6 %attention_backward.1 = (bf16[1,256,768]{2,1,0:T(8,128)(2,1)}, bf16[1,256,128]{2,1,0:T(8,128)(2,1)}, bf16[1,256,128]{2,1,0:T(8,128)(2,1)}, bf16[1,4,128,768]{3,2...) custom-call(bf16[1,256,768]{2,1,0:T(8,128)(2,1)} %q_hbm.1, ...), custom_call_target="tpu_custom_call" | custom-call | tf_op jit(solution)/shard_map/attention_backward/pallas_call | solution.py:561
  58.9 48.8 %emit.1 = (bf16[1,256,768]{2,1,0:T(8,128)(2,1)}, bf16[1,256,128]{2,1,0:T(8,128)(2,1)}, bf16[1,256,128]{2,1,0:T(8,128)(2,1)}, bf16[1,4,128,768]{3,2,1,0:T(8,128)(...) custom-call(bf16[1,256,768]{2,1,0:T(8,128)(2,1)} %get-tuple-element.12.refs_0_, ...), custom_call_target="tpu_custom_call" | custom-call | tf_op jit(solution)/shard_map/emit/pallas_call | solution.py:573

commit v3 on v2

--- a/solution.py
+++ b/solution.py
@@ -20,27 +20,26 @@
 SCALE = 1.0 / math.sqrt(DH)
 SCALE2 = SCALE * math.log2(math.e)
 NEG = -1e30
-ROOT_STEP = 0
 LAST_STEP = 4
 
 HOPS_UP = {
-    (0, 0, 0): (3, 3, 3, 4, 3, 2, 1, 0),
+    (0, 0, 0): (4, 4, 4, 4, 4, 3, 1, 0),
     (0, 0, 1): (0, 0, 0, 0, 0, 4, 4, 4),
-    (0, 1, 0): (0, 0, 3, 4, 3, 2, 4, 4),
-    (0, 1, 1): (4, 3, 4, 3, 4, 3, 4, 3),
-    (1, 0, 0): (4, 4, 4, 4, 4, 4, 4, 4),
-    (1, 0, 1): (0, 0, 0, 0, 0, 4, 4, 4),
-    (1, 1, 0): (4, 3, 4, 3, 4, 3, 4, 3),
+    (0, 1, 0): (0, 0, 0, 0, 0, 1, 1, 3),
+    (0, 1, 1): (3, 3, 3, 3, 3, 0, 1, 2),
+    (1, 0, 0): (4, 4, 3, 3, 4, 4, 4, 4),
+    (1, 0, 1): (0, 0, 0, 0, 0, 3, 3, 4),
+    (1, 1, 0): (0, 3, 4, 3, 3, 2, 4, 4),
     (1, 1, 1): (0, 0, 0, 0, 0, 0, 0, 0),
 }
 HOPS_DOWN = {
-    (0, 0, 0): (4, 4, 4, 0, 0, 0, 0, 0),
+    (0, 0, 0): (3, 3, 3, 0, 3, 0, 0, 0),
     (0, 0, 1): (0, 1, 2, 3, 4, 3, 3, 3),
-    (0, 1, 0): (1, 3, 4, 0, 1, 3, 3, 3),
-    (0, 1, 1): (3, 4, 3, 4, 3, 4, 3, 4),
-    (1, 0, 0): (3, 3, 3, 3, 3, 3, 3, 3),
-    (1, 0, 1): (0, 1, 2, 3, 4, 3, 3, 3),
-    (1, 1, 0): (3, 4, 3, 4, 3, 4, 3, 4),
+    (0, 1, 0): (1, 0, 0, 0, 0, 3, 0, 2),
+    (0, 1, 1): (4, 4, 4, 4, 0, 3, 3, 0),
+    (1, 0, 0): (3, 3, 4, 4, 3, 3, 3, 3),
+    (1, 0, 1): (0, 1, 2, 3, 4, 4, 4, 3),
+    (1, 1, 0): (3, 3, 0, 4, 0, 4, 3, 3),
     (1, 1, 1): (0, 0, 0, 0, 0, 0, 0, 0),
 }
 
@@ -74,8 +73,8 @@
     qs_hbm, ks_hbm, vs_hbm, os_hbm, dos_hbm, slen_ref, scount_ref,
     dq_hbm, dk_hbm, dv_hbm, dqs_hbm, dks_hbm, dvs_hbm,
     kv, q_v, o_v, do_v, scores, ds_v, m_v, l_v, lse_v, delta_v, lo_v, dqt, acc, own,
-    snd, rcv, rcvx, qs_v, ks_v, vs_v, os_v, dos_v, dq_v, dkv_v, dqs_v, dks_v, dvs_v,
-    in_sem, out_sem, ag_send, ag_recv, rs_send, rs_recv, rsx_recv,
+    snd, rcv, qs_v, ks_v, vs_v, os_v, dos_v, dq_v, dkv_v, dqs_v, dks_v, dvs_v,
+    in_sem, out_sem, ag_send, ag_recv, rs_send, rs_recv,
 ):
     f32, bf16 = jnp.float32, jnp.bfloat16
     c = lax.axis_index("ctx")
@@ -87,32 +86,57 @@
     across = (1 - x) * NZ + z
     beside = (x * NZ + z_up, x * NZ + z_down)
 
+    def code(side, direction, foreign, late):
+        table = (HOPS_UP, HOPS_DOWN)[direction]
+        here, there = packed(table[0, foreign, late]), packed(table[1, foreign, late])
+        return jnp.where(x == side, here, there)
+
     codes = [
-        [
-            [jnp.where(x == 1, packed(table[1, foreign, late]), packed(table[0, foreign, late])) for late in (0, 1)]
-            for foreign in (0, 1)
+        [[[code(side, direction, f, l) for l in (0, 1)] for f in (0, 1)] for direction in (0, 1)]
+        for side in (0, 1)
+    ]
+
+    def choose(flag, one, zero):
+        if isinstance(flag, int):
+            return one if flag else zero
+        return jnp.where(flag == 1, one, zero)
+
+    def hops(direction, foreign, late, z_root, side=0):
+        by_late = [
+            [choose(late, codes[side][d][f][1], codes[side][d][f][0]) for f in (0, 1)] for d in (0, 1)
         ]
-        for table in (HOPS_UP, HOPS_DOWN)
-    ]
-
-    def hops(direction, foreign, late, z_root):
-        code = codes[direction][foreign][late]
-        return (code >> (3 * z_root)) & 7
-
-    def hops_dynamic(direction, foreign, late, z_root):
-        by_way = [[jnp.where(direction == 1, codes[1][f][l], codes[0][f][l]) for l in (0, 1)] for f in (0, 1)]
-        by_late = [jnp.where(late == 1, both[1], both[0]) for both in by_way]
-        return (jnp.where(foreign == 1, by_late[1], by_late[0]) >> (3 * z_root)) & 7
+        by_foreign = [choose(foreign, both[1], both[0]) for both in by_late]
+        return (choose(direction, by_foreign[1], by_foreign[0]) >> (3 * z_root)) & 7
 
     def chunk_of(foreign, late, z_root):
         owner = jnp.where(foreign == 1, 1 - x, x) * NZ + z_root
         return jnp.where(late == 1, 2 * NCTX - 1 - owner, owner)
 
-    def early_needs(j):
-        return j <= c
-
-    def late_needs(j):
-        return (j >= 15 - c) & (j <= late_own)
+    def early_needs(j, who=c):
+        return j <= who
+
+    def late_needs(j, who=c):
+        return (j >= 15 - who) & (j <= 2 * NCTX - 1 - who)
+
+    def needs(j, who):
+        return early_needs(j, who) | late_needs(j, who)
+
+    def root_of(way, step):
+        return lax.rem(z + NZ + choose(way, step, -step), NZ)
+
+    def comes_across(late, way, step):
+        z_root = root_of(way, step)
+        j = chunk_of(1, late, z_root)
+        near, far = hops(way, 1, late, z_root), hops(1 - way, 1, late, z_root)
+        there = hops(way, 0, late, z_root, side=1)
+        return (there >= step) & (near < step) & (far < NZ - step) & needs(j, c)
+
+    def goes_across(late, way, step):
+        z_root = root_of(way, step)
+        j = chunk_of(0, late, z_root)
+        near, far = hops(way, 1, late, z_root, side=1), hops(1 - way, 1, late, z_root, side=1)
+        here = hops(way, 0, late, z_root)
+        return (here >= step) & (near < step) & (far < NZ - step) & needs(j, across)
 
     def ag_copy(j, way, target):
         return pltpu.make_async_remote_copy(
@@ -124,12 +148,6 @@
         return pltpu.make_async_remote_copy(
             src_ref=snd.at[j], dst_ref=rcv.at[way, j], send_sem=rs_send.at[j], recv_sem=rs_recv.at[way, j],
             device_id={"ctx": target}, device_id_type=pl.DeviceIdType.MESH,
-        )
-
-    def rsx_copy(j, late):
-        return pltpu.make_async_remote_copy(
-            src_ref=snd.at[j], dst_ref=rcvx.at[late], send_sem=rs_send.at[j], recv_sem=rsx_recv.at[late],
-            device_id={"ctx": across}, device_id_type=pl.DeviceIdType.MESH,
         )
 
     kv_loads = [
@@ -158,10 +176,12 @@
     pl.semaphore_wait(barrier, 3)
 
     def crosses(late):
-        return (x == 1) | (late == 0)
+        on = hops(0, 1, late, z, side=1) + hops(1, 1, late, z, side=1)
+        return (on >= 1) | needs(chunk_of(0, late, z), across)
 
     def arrives(late):
-        return (x == 0) | (late == 0)
+        on = hops(0, 1, late, z) + hops(1, 1, late, z)
+        return (on >= 1) | needs(chunk_of(1, late, z), c)
 
     for copy in kv_loads:
         copy.wait()
@@ -287,11 +307,27 @@
     for copy in short_loads:
         copy.wait()
 
+    def score_across(step):
+        def item(n, carry):
+            late, way = n // 2, lax.rem(n, 2)
+            j = chunk_of(1, late, root_of(way, step))
+
+            @pl.when(comes_across(late, way, step))
+            def _():
+                ag_copy(j, 2, across).wait_recv()
+                score_item(j, c >= 0)
+
+            return carry
+
+        @pl.when(step >= 1)
+        def _():
+            lax.fori_loop(0, 4, item, 0)
+
     def gather_step(step, carry):
         for foreign in (0, 1):
             for late in (0, 1):
                 for way in (0, 1):
-                    z_root = lax.rem(z + NZ + (step if way == 1 else -step), NZ)
+                    z_root = root_of(way, step)
                     j = chunk_of(foreign, late, z_root)
                     reach = hops(way, foreign, late, z_root)
 
@@ -303,17 +339,27 @@
                     def _():
                         ag_copy(j, way, beside[way]).start()
 
-        short_slot(step - 1)
+                    if foreign == 0:
+
+                        @pl.when(goes_across(late, way, step))
+                        def _():
+                            ag_copy(j, 2, across).start()
+
+        @pl.when(step <= SLOTS)
+        def _():
+            short_slot(step - 1)
 
         def item(n, carry):
             foreign, late, way = n // 4, lax.rem(n // 2, 2), lax.rem(n, 2)
-            z_root = lax.rem(z + NZ + jnp.where(way == 1, step, -step), NZ)
-            score_item(chunk_of(foreign, late, z_root), hops_dynamic(way, foreign, late, z_root) >= step)
+            z_root = root_of(way, step)
+            score_item(chunk_of(foreign, late, z_root), hops(way, foreign, late, z_root) >= step)
             return carry
 
-        return lax.fori_loop(0, 8, item, carry)
-
-    lax.fori_loop(1, LAST_STEP + 1, gather_step, 0)
+        lax.fori_loop(0, 8, item, carry)
+        score_across(step - 1)
+        return carry
+
+    lax.fori_loop(1, LAST_STEP + 2, gather_step, 0)
 
     short_stores = [
         pltpu.make_async_copy(src, dst.at[0], out_sem.at[n])
@@ -352,42 +398,64 @@
 
         for_needed(j, c >= 0, grad_tiles)
 
+    def grads_across(step):
+        def item(n, carry):
+            late, way = n // 2, lax.rem(n, 2)
+            j = chunk_of(1, late, root_of(way, step))
+
+            @pl.when(comes_across(late, way, step))
+            def _():
+                grad_item(j)
+                snd[j] = acc[...].astype(bf16)
+                rs_copy(j, 2, across).start()
+
+            return carry
+
+        @pl.when(step >= 1)
+        def _():
+            lax.fori_loop(0, 4, item, 0)
+
+    def add_term(way, j, target):
+        rs_copy(j, way, target).wait_recv()
+        acc[...] += rcv[way, j].astype(f32)
+
     def scatter_step(back, carry):
-        step = LAST_STEP - back
+        step = LAST_STEP + 1 - back
+        grads_across(step - 1)
 
         def item(n, carry):
             foreign, late, way = n // 4, lax.rem(n // 2, 2), lax.rem(n, 2)
-            z_root = lax.rem(z + NZ + jnp.where(way == 1, step, -step), NZ)
+            z_root = root_of(way, step)
             j = chunk_of(foreign, late, z_root)
-            reach = hops_dynamic(way, foreign, late, z_root)
+            reach = hops(way, foreign, late, z_root)
 
             @pl.when(reach >= step)
             def _():
                 grad_item(j)
-                home = jnp.where(way == 1, beside[0], beside[1])
-                copy = rs_copy(j, way, home)
 
                 @pl.when(reach >= step + 1)
                 def _():
-                    copy.wait_recv()
-                    acc[...] += rcv[way, j].astype(f32)
+                    add_term(way, j, beside[0])
+
+                @pl.when((foreign == 0) & goes_across(late, way, step))
+                def _():
+                    add_term(2, j, across)
 
                 snd[j] = acc[...].astype(bf16)
-                copy.start()
+                rs_copy(j, way, choose(way, beside[0], beside[1])).start()
 
             return carry
 
         return lax.fori_loop(0, 8, item, carry)
 
-    lax.fori_loop(0, LAST_STEP, scatter_step, 0)
+    lax.fori_loop(0, LAST_STEP + 1, scatter_step, 0)
 
     def collect(foreign, late, j):
         for way in (0, 1):
 
-            @pl.when(hops_dynamic(way, foreign, late, z) >= 1)
-            def _():
-                rs_copy(j, way, beside[way]).wait_recv()
-                acc[...] += rcv[way, j].astype(f32)
+            @pl.when(hops(way, foreign, late, z) >= 1)
+            def _():
+                add_term(way, j, beside[way])
 
     def foreign_root(late, carry):
         j = chunk_of(1, late, z)
@@ -397,7 +465,7 @@
             grad_item(j)
             collect(1, late, j)
             snd[j] = acc[...].astype(bf16)
-            rsx_copy(j, late).start()
+            rs_copy(j, 2, across).start()
 
         return carry
 
@@ -446,8 +514,7 @@
 
         @pl.when(crosses(late))
         def _():
-            rsx_copy(j, late).wait_recv()
-            acc[...] += rcvx[late].astype(f32)
+            add_term(2, j, across)
 
         rows = pl.ds(pl.multiple_of(late * CH, CH), CH)
         dkv_v[0, rows] = (acc[0] * SCALE).astype(bf16)
@@ -478,14 +545,14 @@
 
         @pl.when(arrives(late))
         def _():
-            rsx_copy(chunk_of(1, late, z), late).wait_send()
+            rs_copy(chunk_of(1, late, z), 2, across).wait_send()
 
     def sent_step(step, carry):
         def item(n, carry):
             foreign, late, way = n // 4, lax.rem(n // 2, 2), lax.rem(n, 2)
-            z_root = lax.rem(z + NZ + jnp.where(way == 1, step, -step), NZ)
+            z_root = root_of(way, step)
             j = chunk_of(foreign, late, z_root)
-            reach = hops_dynamic(way, foreign, late, z_root)
+            reach = hops(way, foreign, late, z_root)
 
             @pl.when(reach >= step)
             def _():
@@ -494,6 +561,14 @@
             @pl.when(reach >= step + 1)
             def _():
                 ag_copy(j, way, beside[0]).wait_send()
+
+            @pl.when((foreign == 0) & goes_across(late, way, step))
+            def _():
+                ag_copy(j, 2, across).wait_send()
+
+            @pl.when((foreign == 1) & comes_across(late, way, step))
+            def _():
+                rs_copy(j, 2, across).wait_send()
 
             return carry
 
@@ -506,12 +581,16 @@
 
 
 def emit(*refs):
-    sem = refs[12]
-    copies = [pltpu.make_async_copy(refs[n], refs[6 + n], sem.at[n]) for n in range(6)]
-    for copy in copies:
-        copy.start()
-    for copy in copies:
-        copy.wait()
+    ins, outs, held, in_sem, out_sem = refs[:6], refs[6:12], refs[12:18], refs[18], refs[19]
+    loads = [pltpu.make_async_copy(ins[n], held[n], in_sem.at[n]) for n in range(6)]
+    stores = [pltpu.make_async_copy(held[n], outs[n], out_sem.at[n]) for n in range(6)]
+    for load in loads:
+        load.start()
+    for load, store in zip(loads, stores):
+        load.wait()
+        store.start()
+    for store in stores:
+        store.wait()
 
 
 def body(*args):
@@ -538,8 +617,7 @@
         pltpu.VMEM((2, CH, DH), f32),
         pltpu.VMEM((2, 2, CH, DH), f32),
         pltpu.VMEM((NCHUNK, 2, CH, DH), bf16),
-        pltpu.VMEM((2, NCHUNK, 2, CH, DH), bf16),
-        pltpu.VMEM((2, 2, CH, DH), bf16),
+        pltpu.VMEM((3, NCHUNK, 2, CH, DH), bf16),
         pltpu.VMEM((SLOTS, CH, HC), bf16),
         pltpu.VMEM((SLOTS, CH, DH), bf16),
         pltpu.VMEM((SLOTS, CH, DH), bf16),
@@ -555,8 +633,7 @@
         dma((NCHUNK, 3)),
         dma((NCHUNK,)),
         dma((NCHUNK,)),
-        dma((2, NCHUNK)),
-        dma((2,)),
+        dma((3, NCHUNK)),
     ]
     grads = pl.pallas_call(
         kernel,
@@ -575,7 +652,7 @@
             out_shape=out_shape,
             in_specs=[any_spec] * 6,
             out_specs=[any_spec] * 6,
-            scratch_shapes=[dma((6,))],
+            scratch_shapes=[pltpu.VMEM(out.shape, bf16) for out in out_shape] + [dma((6,)), dma((6,))],
             compiler_params=pltpu.CompilerParams(vmem_limit_bytes=60 * 1024 * 1024),
             name="emit",
         )(*grads)

time: 109 us -> 68.1 us (0.62)
  Pallas kernels: 106 us -> 66.1 us
    pallas_call x1, Pallas kernels: 48.8 us -> 2.38 us  [body(): pl.pallas_call(emit, out_shape=out_shape, in_specs=[any_spec] * 6, out_sp...]
    pallas_call x1, Pallas kernels: 57.6 us -> 63.8 us  [body(): pl.pallas_call(kernel, out_shape=out_shape, in_specs=in_specs, out_specs=...]
where the time goes in v3:
time: 68.1 us; the launch traced here: 67.4 us
  Pallas kernels  66.1 us (97%)
  between operations  1.29 us (2%)
    pallas_call x1, Pallas kernels, body(): pl.pallas_call(kernel, out_shape=out_shape, in_specs=in_specs, out_specs=...  63.8 us
    pallas_call x1, Pallas kernels, body(): pl.pallas_call(emit, out_shape=out_shape, in_specs=[any_spec] * 6, out_sp...  2.38 us

profile of v3, /device:TPU:8, one launch (start us, length us, event | category | flops | bytes accessed | tf_op | source)
XLA Modules:
  0.0 67.4 jit_solution(9111549361463985933)
XLA Ops:
  1.3 63.8 %attention_backward.1 = (bf16[1,256,768]{2,1,0:T(8,128)(2,1)}, bf16[1,256,128]{2,1,0:T(8,128)(2,1)}, bf16[1,256,128]{2,1,0:T(8,128)(2,1)}, bf16[1,4,128,768]{3,2...) custom-call(bf16[1,256,768]{2,1,0:T(8,128)(2,1)} %q_hbm.1, ...), custom_call_target="tpu_custom_call" | custom-call | tf_op jit(solution)/shard_map/attention_backward/pallas_call | solution.py:638
  65.1 2.4 %emit.1 = (bf16[1,256,768]{2,1,0:T(8,128)(2,1)}, bf16[1,256,128]{2,1,0:T(8,128)(2,1)}, bf16[1,256,128]{2,1,0:T(8,128)(2,1)}, bf16[1,4,128,768]{3,2,1,0:T(8,128)(...) custom-call(bf16[1,256,768]{2,1,0:T(8,128)(2,1)} %get-tuple-element.12.refs_0_, ...), custom_call_target="tpu_custom_call" | custom-call | tf_op jit(solution)/shard_map/emit/pallas_call | solution.py:650

commit v4 on v3

--- a/solution.py
+++ b/solution.py
@@ -23,29 +23,68 @@
 LAST_STEP = 4
 
 HOPS_UP = {
-    (0, 0, 0): (4, 4, 4, 4, 4, 3, 1, 0),
+    (0, 0, 0): (3, 3, 3, 4, 3, 2, 1, 0),
     (0, 0, 1): (0, 0, 0, 0, 0, 4, 4, 4),
-    (0, 1, 0): (0, 0, 0, 0, 0, 1, 1, 3),
-    (0, 1, 1): (3, 3, 3, 3, 3, 0, 1, 2),
-    (1, 0, 0): (4, 4, 3, 3, 4, 4, 4, 4),
-    (1, 0, 1): (0, 0, 0, 0, 0, 3, 3, 4),
-    (1, 1, 0): (0, 3, 4, 3, 3, 2, 4, 4),
+    (0, 1, 0): (0, 0, 3, 4, 3, 2, 4, 4),
+    (0, 1, 1): (4, 3, 4, 3, 4, 3, 4, 3),
+    (1, 0, 0): (4, 4, 4, 4, 4, 4, 4, 4),
+    (1, 0, 1): (0, 0, 0, 0, 0, 4, 4, 4),
+    (1, 1, 0): (4, 3, 4, 3, 4, 3, 4, 3),
     (1, 1, 1): (0, 0, 0, 0, 0, 0, 0, 0),
 }
 HOPS_DOWN = {
-    (0, 0, 0): (3, 3, 3, 0, 3, 0, 0, 0),
+    (0, 0, 0): (4, 4, 4, 0, 0, 0, 0, 0),
     (0, 0, 1): (0, 1, 2, 3, 4, 3, 3, 3),
-    (0, 1, 0): (1, 0, 0, 0, 0, 3, 0, 2),
-    (0, 1, 1): (4, 4, 4, 4, 0, 3, 3, 0),
-    (1, 0, 0): (3, 3, 4, 4, 3, 3, 3, 3),
-    (1, 0, 1): (0, 1, 2, 3, 4, 4, 4, 3),
-    (1, 1, 0): (3, 3, 0, 4, 0, 4, 3, 3),
+    (0, 1, 0): (1, 3, 4, 0, 1, 3, 3, 3),
+    (0, 1, 1): (3, 4, 3, 4, 3, 4, 3, 4),
+    (1, 0, 0): (3, 3, 3, 3, 3, 3, 3, 3),
+    (1, 0, 1): (0, 1, 2, 3, 4, 3, 3, 3),
+    (1, 1, 0): (3, 4, 3, 4, 3, 4, 3, 4),
     (1, 1, 1): (0, 0, 0, 0, 0, 0, 0, 0),
 }
 
 
-def packed(hops):
-    return sum(h << (3 * z) for z, h in enumerate(hops))
+def needed(j, c):
+    return j <= c or 15 - c <= j <= 31 - c
+
+
+def device_masks(c):
+    x, z = divmod(c, NZ)
+    across = (1 - x) * NZ + z
+    hops = (HOPS_UP, HOPS_DOWN)
+
+    def chunk(plane, late, zr):
+        owner = plane * NZ + zr
+        return 2 * NCTX - 1 - owner if late else owner
+
+    def over_x(plane, late, way, step, to):
+        zr = (z + step if way else z - step) % NZ
+        near, far = hops[way][1 - plane, 1, late][zr], hops[1 - way][1 - plane, 1, late][zr]
+        there = hops[way][plane, 0, late][zr]
+        return there >= step and near < step and far < NZ - step and needed(chunk(plane, late, zr), to)
+
+    def root_over_x(plane, late, to):
+        on = hops[0][1 - plane, 1, late][z] + hops[1][1 - plane, 1, late][z]
+        return on >= 1 or needed(chunk(plane, late, z), to)
+
+    has = forwards = over = root = 0
+    for late in (0, 1):
+        root |= root_over_x(x, late, across) << late
+        root |= root_over_x(1 - x, late, c) << (2 + late)
+        for way in (0, 1):
+            for foreign in (0, 1):
+                n = 4 * foreign + 2 * late + way
+                root |= (hops[way][x, foreign, late][z] >= 1) << (4 + n)
+                for step in range(1, LAST_STEP + 1):
+                    zr = (z + step if way else z - step) % NZ
+                    reach = hops[way][x, foreign, late][zr]
+                    has |= (reach >= step) << (8 * (step - 1) + n)
+                    forwards |= (reach >= step + 1) << (8 * (step - 1) + n)
+            for step in range(1, LAST_STEP + 1):
+                bit = 4 * (step - 1) + 2 * late + way
+                over |= over_x(x, late, way, step, across) << bit
+                over |= over_x(1 - x, late, way, step, c) << (16 + bit)
+    return tuple(m - (1 << 32) if m >= 1 << 31 else m for m in (has, forwards, over, root))
 
 
 def nt(a, b):
@@ -72,7 +111,7 @@
     q_hbm, k_hbm, v_hbm, o_hbm, do_hbm, doc_ref,
     qs_hbm, ks_hbm, vs_hbm, os_hbm, dos_hbm, slen_ref, scount_ref,
     dq_hbm, dk_hbm, dv_hbm, dqs_hbm, dks_hbm, dvs_hbm,
-    kv, q_v, o_v, do_v, scores, ds_v, m_v, l_v, lse_v, delta_v, lo_v, dqt, acc, own,
+    kv, q_v, o_v, do_v, qt_v, dot_v, scores, ds_v, m_v, l_v, lse_v, delta_v, lo_v, dqt, acc, own,
     snd, rcv, qs_v, ks_v, vs_v, os_v, dos_v, dq_v, dkv_v, dqs_v, dks_v, dvs_v,
     in_sem, out_sem, ag_send, ag_recv, rs_send, rs_recv,
 ):
@@ -86,57 +125,53 @@
     across = (1 - x) * NZ + z
     beside = (x * NZ + z_up, x * NZ + z_down)
 
-    def code(side, direction, foreign, late):
-        table = (HOPS_UP, HOPS_DOWN)[direction]
-        here, there = packed(table[0, foreign, late]), packed(table[1, foreign, late])
-        return jnp.where(x == side, here, there)
-
-    codes = [
-        [[[code(side, direction, f, l) for l in (0, 1)] for f in (0, 1)] for direction in (0, 1)]
-        for side in (0, 1)
-    ]
+    masks = [jnp.int32(m) for m in device_masks(0)]
+    for device in range(1, NCTX):
+        here = c == device
+        masks = [jnp.where(here, jnp.int32(m), old) for m, old in zip(device_masks(device), masks)]
+    has_mask, forward_mask, over_mask, root_mask = masks
+
+    def bit(mask, n):
+        return ((mask >> n) & 1) == 1
+
+    def has(step, n):
+        return bit(has_mask, 8 * (step - 1) + n)
+
+    def forwards(step, n):
+        return bit(forward_mask, 8 * (step - 1) + n)
+
+    def goes_across(step, n):
+        return bit(over_mask, 4 * (step - 1) + n)
+
+    def comes_across(step, n):
+        return bit(over_mask, 16 + 4 * (step - 1) + n)
+
+    def crosses(late):
+        return bit(root_mask, late)
+
+    def arrives(late):
+        return bit(root_mask, 2 + late)
+
+    def sets_out(foreign, late, way):
+        return bit(root_mask, 4 + 4 * foreign + 2 * late + way)
 
     def choose(flag, one, zero):
         if isinstance(flag, int):
             return one if flag else zero
         return jnp.where(flag == 1, one, zero)
 
-    def hops(direction, foreign, late, z_root, side=0):
-        by_late = [
-            [choose(late, codes[side][d][f][1], codes[side][d][f][0]) for f in (0, 1)] for d in (0, 1)
-        ]
-        by_foreign = [choose(foreign, both[1], both[0]) for both in by_late]
-        return (choose(direction, by_foreign[1], by_foreign[0]) >> (3 * z_root)) & 7
-
     def chunk_of(foreign, late, z_root):
-        owner = jnp.where(foreign == 1, 1 - x, x) * NZ + z_root
-        return jnp.where(late == 1, 2 * NCTX - 1 - owner, owner)
+        owner = (x + foreign * (1 - 2 * x)) * NZ + z_root
+        return owner + late * (2 * NCTX - 1 - 2 * owner)
+
+    def root_of(way, step):
+        return (z + NZ + step * (2 * way - 1)) & (NZ - 1)
 
     def early_needs(j, who=c):
         return j <= who
 
     def late_needs(j, who=c):
         return (j >= 15 - who) & (j <= 2 * NCTX - 1 - who)
-
-    def needs(j, who):
-        return early_needs(j, who) | late_needs(j, who)
-
-    def root_of(way, step):
-        return lax.rem(z + NZ + choose(way, step, -step), NZ)
-
-    def comes_across(late, way, step):
-        z_root = root_of(way, step)
-        j = chunk_of(1, late, z_root)
-        near, far = hops(way, 1, late, z_root), hops(1 - way, 1, late, z_root)
-        there = hops(way, 0, late, z_root, side=1)
-        return (there >= step) & (near < step) & (far < NZ - step) & needs(j, c)
-
-    def goes_across(late, way, step):
-        z_root = root_of(way, step)
-        j = chunk_of(0, late, z_root)
-        near, far = hops(way, 1, late, z_root, side=1), hops(1 - way, 1, late, z_root, side=1)
-        here = hops(way, 0, late, z_root)
-        return (here >= step) & (near < step) & (far < NZ - step) & needs(j, across)
 
     def ag_copy(j, way, target):
         return pltpu.make_async_remote_copy(
@@ -175,14 +210,6 @@
         )
     pl.semaphore_wait(barrier, 3)
 
-    def crosses(late):
-        on = hops(0, 1, late, z, side=1) + hops(1, 1, late, z, side=1)
-        return (on >= 1) | needs(chunk_of(0, late, z), across)
-
-    def arrives(late):
-        on = hops(0, 1, late, z) + hops(1, 1, late, z)
-        return (on >= 1) | needs(chunk_of(1, late, z), c)
-
     for copy in kv_loads:
         copy.wait()
     for late in (0, 1):
@@ -196,7 +223,7 @@
         j = chunk_of(0, late, z)
         for way in (0, 1):
 
-            @pl.when(hops(way, 0, late, z) >= 1)
+            @pl.when(sets_out(0, late, way))
             def _():
                 ag_copy(j, way, beside[way]).start()
 
@@ -219,6 +246,9 @@
         lo_v[half] = first
         for col in PAIRS:
             delta_v[half, :, col : col + 2 * DH] = row_delta(heads(do_v.at[rows], col), heads(o_v.at[rows], col))
+        for col in range(0, HC, DH):
+            qt_v[half, :, col : col + DH] = q_v[rows, col : col + DH].T
+            dot_v[half, :, col : col + DH] = do_v[rows, col : col + DH].T
         m_v[half] = jnp.full((8, HC), NEG, f32)
         l_v[half] = jnp.zeros((8, HC), f32)
     dqt[0] = jnp.zeros((DH, HC), f32)
@@ -230,13 +260,13 @@
         keys = kv[j, 0]
         key_pos = j * CH + sub
         for half in which:
-            rows, own_chunk = halves[half]
+            own_chunk = halves[half][1]
             visible = (key_pos >= lo_v[half]) & (key_pos <= own_chunk * CH + lane)
             bias = jnp.where(visible, 0.0, NEG)
             slot = slot_of(half, j)
             for col in PAIRS:
                 cols = slice(col, col + 2 * DH)
-                s = nt(keys, heads(q_v.at[rows], col)) * SCALE2 + bias
+                s = nn(keys, qt_v[half, :, cols]) * SCALE2 + bias
                 scores[slot, :, cols] = s
                 s = s.reshape(CH // 8, 8, 2 * DH)
                 m_old = m_v[half, :, cols]
@@ -294,7 +324,7 @@
             ag_copy(j, 2, across).wait_recv()
             for way in (0, 1):
 
-                @pl.when(hops(way, 1, late, z) >= 1)
+                @pl.when(sets_out(1, late, way))
                 def _():
                     ag_copy(j, way, beside[way]).start()
 
@@ -309,10 +339,9 @@
 
     def score_across(step):
         def item(n, carry):
-            late, way = n // 2, lax.rem(n, 2)
-            j = chunk_of(1, late, root_of(way, step))
-
-            @pl.when(comes_across(late, way, step))
+            j = chunk_of(1, n // 2, root_of(lax.rem(n, 2), step))
+
+            @pl.when(comes_across(step, n))
             def _():
                 ag_copy(j, 2, across).wait_recv()
                 score_item(j, c >= 0)
@@ -324,42 +353,37 @@
             lax.fori_loop(0, 4, item, 0)
 
     def gather_step(step, carry):
-        for foreign in (0, 1):
-            for late in (0, 1):
-                for way in (0, 1):
-                    z_root = root_of(way, step)
-                    j = chunk_of(foreign, late, z_root)
-                    reach = hops(way, foreign, late, z_root)
-
-                    @pl.when(reach >= step)
-                    def _():
-                        ag_copy(j, way, beside[way]).wait_recv()
-
-                    @pl.when(reach >= step + 1)
-                    def _():
-                        ag_copy(j, way, beside[way]).start()
-
-                    if foreign == 0:
-
-                        @pl.when(goes_across(late, way, step))
-                        def _():
-                            ag_copy(j, 2, across).start()
-
-        @pl.when(step <= SLOTS)
-        def _():
-            short_slot(step - 1)
+        for n in range(8):
+            foreign, late, way = n // 4, n // 2 % 2, n % 2
+            j = chunk_of(foreign, late, root_of(way, step))
+
+            @pl.when(has(step, n))
+            def _():
+                ag_copy(j, way, beside[way]).wait_recv()
+
+            @pl.when(forwards(step, n))
+            def _():
+                ag_copy(j, way, beside[way]).start()
+
+            if foreign == 0:
+
+                @pl.when(goes_across(step, n))
+                def _():
+                    ag_copy(j, 2, across).start()
+
+        short_slot(step - 1)
 
         def item(n, carry):
-            foreign, late, way = n // 4, lax.rem(n // 2, 2), lax.rem(n, 2)
-            z_root = root_of(way, step)
-            score_item(chunk_of(foreign, late, z_root), hops(way, foreign, late, z_root) >= step)
+            foreign, late, way = n // 4, (n // 2) & 1, n & 1
+            score_item(chunk_of(foreign, late, root_of(way, step)), has(step, n))
             return carry
 
         lax.fori_loop(0, 8, item, carry)
         score_across(step - 1)
         return carry
 
-    lax.fori_loop(1, LAST_STEP + 2, gather_step, 0)
+    lax.fori_loop(1, LAST_STEP + 1, gather_step, 0)
+    score_across(LAST_STEP)
 
     short_stores = [
         pltpu.make_async_copy(src, dst.at[0], out_sem.at[n])
@@ -382,7 +406,7 @@
                 cols = slice(col, col + 2 * DH)
                 grads = heads(do_v.at[rows], col)
                 p = jnp.exp2(scores[slot, :, cols] - lse_v[half, :, cols])
-                ds = (p * (nt(values, grads) - delta_v[half, :, cols])).astype(bf16)
+                ds = (p * (nn(values, dot_v[half, :, cols]) - delta_v[half, :, cols])).astype(bf16)
                 ds_v[slot, :, cols] = ds
                 p_parts.append(p.astype(bf16))
                 ds_parts.append(ds)
@@ -400,10 +424,9 @@
 
     def grads_across(step):
         def item(n, carry):
-            late, way = n // 2, lax.rem(n, 2)
-            j = chunk_of(1, late, root_of(way, step))
-
-            @pl.when(comes_across(late, way, step))
+            j = chunk_of(1, n // 2, root_of(lax.rem(n, 2), step))
+
+            @pl.when(comes_across(step, n))
             def _():
                 grad_item(j)
                 snd[j] = acc[...].astype(bf16)
@@ -420,24 +443,22 @@
         acc[...] += rcv[way, j].astype(f32)
 
     def scatter_step(back, carry):
-        step = LAST_STEP + 1 - back
+        step = LAST_STEP - back
         grads_across(step - 1)
 
         def item(n, carry):
-            foreign, late, way = n // 4, lax.rem(n // 2, 2), lax.rem(n, 2)
-            z_root = root_of(way, step)
-            j = chunk_of(foreign, late, z_root)
-            reach = hops(way, foreign, late, z_root)
-
-            @pl.when(reach >= step)
+            foreign, late, way = n // 4, (n // 2) & 1, n & 1
+            j = chunk_of(foreign, late, root_of(way, step))
+
+            @pl.when(has(step, n))
             def _():
                 grad_item(j)
 
-                @pl.when(reach >= step + 1)
+                @pl.when(forwards(step, n))
                 def _():
                     add_term(way, j, beside[0])
 
-                @pl.when((foreign == 0) & goes_across(late, way, step))
+                @pl.when((foreign == 0) & goes_across(step, n & 3))
                 def _():
                     add_term(2, j, across)
 
@@ -448,12 +469,13 @@
 
         return lax.fori_loop(0, 8, item, carry)
 
-    lax.fori_loop(0, LAST_STEP + 1, scatter_step, 0)
+    grads_across(LAST_STEP)
+    lax.fori_loop(0, LAST_STEP, scatter_step, 0)
 
     def collect(foreign, late, j):
         for way in (0, 1):
 
-            @pl.when(hops(way, foreign, late, z) >= 1)
+            @pl.when(sets_out(foreign, late, way))
             def _():
                 add_term(way, j, beside[way])
 
@@ -507,6 +529,54 @@
     dq_store = pltpu.make_async_copy(dq_v, dq_hbm.at[0], out_sem.at[3])
     dq_store.start()
 
+    for late in (0, 1):
+        j = chunk_of(0, late, z)
+
+        @pl.when(crosses(late))
+        def _():
+            ag_copy(j, 2, across).wait_send()
+
+        for foreign in (0, 1):
+            j = chunk_of(foreign, late, z)
+            for way in (0, 1):
+
+                @pl.when(sets_out(foreign, late, way))
+                def _():
+                    ag_copy(j, way, beside[way]).wait_send()
+
+        @pl.when(arrives(late))
+        def _():
+            rs_copy(chunk_of(1, late, z), 2, across).wait_send()
+
+    def sent_step(step, carry):
+        for n in range(8):
+            foreign, late, way = n // 4, n // 2 % 2, n % 2
+            j = chunk_of(foreign, late, root_of(way, step))
+
+            @pl.when(has(step, n))
+            def _():
+                rs_copy(j, way, beside[0]).wait_send()
+
+            @pl.when(forwards(step, n))
+            def _():
+                ag_copy(j, way, beside[0]).wait_send()
+
+            if foreign == 0:
+
+                @pl.when(goes_across(step, n))
+                def _():
+                    ag_copy(j, 2, across).wait_send()
+
+            else:
+
+                @pl.when(comes_across(step, n & 3))
+                def _():
+                    rs_copy(j, 2, across).wait_send()
+
+        return carry
+
+    lax.fori_loop(1, LAST_STEP + 1, sent_step, 0)
+
     def own_total(late, carry):
         acc[...] = own[late]
         j = chunk_of(0, late, z)
@@ -527,54 +597,6 @@
     ]
     for copy in kv_stores:
         copy.start()
-
-    for late in (0, 1):
-        j = chunk_of(0, late, z)
-
-        @pl.when(crosses(late))
-        def _():
-            ag_copy(j, 2, across).wait_send()
-
-        for foreign in (0, 1):
-            j = chunk_of(foreign, late, z)
-            for way in (0, 1):
-
-                @pl.when(hops(way, foreign, late, z) >= 1)
-                def _():
-                    ag_copy(j, way, beside[way]).wait_send()
-
-        @pl.when(arrives(late))
-        def _():
-            rs_copy(chunk_of(1, late, z), 2, across).wait_send()
-
-    def sent_step(step, carry):
-        def item(n, carry):
-            foreign, late, way = n // 4, lax.rem(n // 2, 2), lax.rem(n, 2)
-            z_root = root_of(way, step)
-            j = chunk_of(foreign, late, z_root)
-            reach = hops(way, foreign, late, z_root)
-
-            @pl.when(reach >= step)
-            def _():
-                rs_copy(j, way, beside[0]).wait_send()
-
-            @pl.when(reach >= step + 1)
-            def _():
-                ag_copy(j, way, beside[0]).wait_send()
-
-            @pl.when((foreign == 0) & goes_across(late, way, step))
-            def _():
-                ag_copy(j, 2, across).wait_send()
-
-            @pl.when((foreign == 1) & comes_across(late, way, step))
-            def _():
-                rs_copy(j, 2, across).wait_send()
-
-            return carry
-
-        return lax.fori_loop(0, 8, item, carry)
-
-    lax.fori_loop(1, LAST_STEP + 1, sent_step, 0)
 
     for copy in short_stores + [dq_store] + kv_stores:
         copy.wait()
@@ -606,6 +628,8 @@
         pltpu.VMEM((tok, HC), bf16),
         pltpu.VMEM((tok, HC), bf16),
         pltpu.VMEM((tok, HC), bf16),
+        pltpu.VMEM((2, DH, HC), bf16),
+        pltpu.VMEM((2, DH, HC), bf16),
         pltpu.VMEM((33, CH, HC), f32),
         pltpu.VMEM((33, CH, HC), bf16),
         pltpu.VMEM((2, 8, HC), f32),

time: 68.1 us -> 61.6 us (0.905)
  Pallas kernels: 66.1 us -> 59.6 us
    pallas_call x1, Pallas kernels: 63.8 us -> 57.2 us  [body(): pl.pallas_call(kernel, out_shape=out_shape, in_specs=in_specs, out_specs=...]
where the time goes in v4:
time: 61.6 us; the launch traced here: 60.9 us
  Pallas kernels  59.6 us (97%)
  between operations  1.29 us (2%)
    pallas_call x1, Pallas kernels, body(): pl.pallas_call(kernel, out_shape=out_shape, in_specs=in_specs, out_specs=...  57.2 us
    pallas_call x1, Pallas kernels, body(): pl.pallas_call(emit, out_shape=out_shape, in_specs=[any_spec] * 6, out_sp...  2.38 us

profile of v4, /device:TPU:8, one launch (start us, length us, event | category | flops | bytes accessed | tf_op | source)
XLA Modules:
  0.0 60.9 jit_solution(2298450731704000027)
XLA Ops:
  1.3 57.2 %attention_backward.1 = (bf16[1,256,768]{2,1,0:T(8,128)(2,1)}, bf16[1,256,128]{2,1,0:T(8,128)(2,1)}, bf16[1,256,128]{2,1,0:T(8,128)(2,1)}, bf16[1,4,128,768]{3,2...) custom-call(bf16[1,256,768]{2,1,0:T(8,128)(2,1)} %q_hbm.1, ...), custom_call_target="tpu_custom_call" | custom-call | tf_op jit(solution)/shard_map/attention_backward/pallas_call | solution.py:662
  58.5 2.4 %emit.1 = (bf16[1,256,768]{2,1,0:T(8,128)(2,1)}, bf16[1,256,128]{2,1,0:T(8,128)(2,1)}, bf16[1,256,128]{2,1,0:T(8,128)(2,1)}, bf16[1,4,128,768]{3,2,1,0:T(8,128)(...) custom-call(bf16[1,256,768]{2,1,0:T(8,128)(2,1)} %get-tuple-element.12.refs_0_, ...), custom_call_target="tpu_custom_call" | custom-call | tf_op jit(solution)/shard_map/emit/pallas_call | solution.py:674

commit v5 on v4

--- a/solution.py
+++ b/solution.py
@@ -23,23 +23,23 @@
 LAST_STEP = 4
 
 HOPS_UP = {
-    (0, 0, 0): (3, 3, 3, 4, 3, 2, 1, 0),
-    (0, 0, 1): (0, 0, 0, 0, 0, 4, 4, 4),
-    (0, 1, 0): (0, 0, 3, 4, 3, 2, 4, 4),
-    (0, 1, 1): (4, 3, 4, 3, 4, 3, 4, 3),
-    (1, 0, 0): (4, 4, 4, 4, 4, 4, 4, 4),
-    (1, 0, 1): (0, 0, 0, 0, 0, 4, 4, 4),
-    (1, 1, 0): (4, 3, 4, 3, 4, 3, 4, 3),
+    (0, 0, 0): (3, 3, 4, 4, 3, 2, 1, 0),
+    (0, 0, 1): (0, 0, 0, 0, 0, 3, 4, 4),
+    (0, 1, 0): (0, 0, 4, 4, 0, 0, 0, 4),
+    (0, 1, 1): (1, 4, 1, 3, 4, 4, 3, 4),
+    (1, 0, 0): (4, 4, 4, 3, 4, 3, 4, 4),
+    (1, 0, 1): (3, 0, 3, 0, 0, 3, 3, 3),
+    (1, 1, 0): (4, 3, 3, 4, 3, 4, 4, 3),
     (1, 1, 1): (0, 0, 0, 0, 0, 0, 0, 0),
 }
 HOPS_DOWN = {
-    (0, 0, 0): (4, 4, 4, 0, 0, 0, 0, 0),
-    (0, 0, 1): (0, 1, 2, 3, 4, 3, 3, 3),
-    (0, 1, 0): (1, 3, 4, 0, 1, 3, 3, 3),
-    (0, 1, 1): (3, 4, 3, 4, 3, 4, 3, 4),
-    (1, 0, 0): (3, 3, 3, 3, 3, 3, 3, 3),
-    (1, 0, 1): (0, 1, 2, 3, 4, 3, 3, 3),
-    (1, 1, 0): (3, 4, 3, 4, 3, 4, 3, 4),
+    (0, 0, 0): (4, 4, 3, 0, 0, 0, 3, 0),
+    (0, 0, 1): (0, 1, 2, 3, 4, 4, 3, 3),
+    (0, 1, 0): (1, 3, 0, 0, 1, 0, 4, 2),
+    (0, 1, 1): (4, 3, 4, 4, 3, 3, 4, 1),
+    (1, 0, 0): (3, 3, 3, 4, 3, 4, 3, 3),
+    (1, 0, 1): (0, 1, 2, 3, 4, 4, 4, 4),
+    (1, 1, 0): (3, 4, 4, 3, 4, 3, 0, 4),
     (1, 1, 1): (0, 0, 0, 0, 0, 0, 0, 0),
 }
 
@@ -110,10 +110,10 @@
 def kernel(
     q_hbm, k_hbm, v_hbm, o_hbm, do_hbm, doc_ref,
     qs_hbm, ks_hbm, vs_hbm, os_hbm, dos_hbm, slen_ref, scount_ref,
-    dq_hbm, dk_hbm, dv_hbm, dqs_hbm, dks_hbm, dvs_hbm,
-    kv, q_v, o_v, do_v, qt_v, dot_v, scores, ds_v, m_v, l_v, lse_v, delta_v, lo_v, dqt, acc, own,
-    snd, rcv, qs_v, ks_v, vs_v, os_v, dos_v, dq_v, dkv_v, dqs_v, dks_v, dvs_v,
-    in_sem, out_sem, ag_send, ag_recv, rs_send, rs_recv,
+    dq_out, dk_out, dv_out, dqs_out, dks_out, dvs_out,
+    kv, q_v, o_v, do_v, qt_v, dot_v, scores, ds_v, m_v, l_v, lse_v, delta_v, lo_v, dqt, acc, held,
+    snd, rcv, qs_v, ks_v, vs_v, os_v, dos_v,
+    in_sem, ag_send, ag_recv, rs_send, rs_recv,
 ):
     f32, bf16 = jnp.float32, jnp.bfloat16
     c = lax.axis_index("ctx")
@@ -307,11 +307,11 @@
             dk = dk + nn(ds, queries)
             dq = lax.dot_general(keys, ds, (((0,), (0,)), ((), ())), preferred_element_type=f32)
             for n in (0, 1):
-                dqs_v[slot, :, col + n * DH : col + (n + 1) * DH] = (
+                dqs_out[0, slot, :, col + n * DH : col + (n + 1) * DH] = (
                     dq[:, n * DH : (n + 1) * DH].T * SCALE
                 ).astype(bf16)
-        dks_v[slot] = (dk * SCALE).astype(bf16)
-        dvs_v[slot] = dv.astype(bf16)
+        dks_out[0, slot] = (dk * SCALE).astype(bf16)
+        dvs_out[0, slot] = dv.astype(bf16)
 
     score_item(c, c >= 0)
     score_item(late_own, c >= 0)
@@ -384,13 +384,6 @@
 
     lax.fori_loop(1, LAST_STEP + 1, gather_step, 0)
     score_across(LAST_STEP)
-
-    short_stores = [
-        pltpu.make_async_copy(src, dst.at[0], out_sem.at[n])
-        for n, (src, dst) in enumerate(((dqs_v, dqs_hbm), (dks_v, dks_hbm), (dvs_v, dvs_hbm)))
-    ]
-    for copy in short_stores:
-        copy.start()
 
     for half in (0, 1):
         m = jnp.max(m_v[half], axis=0, keepdims=True)
@@ -442,11 +435,27 @@
         rs_copy(j, way, target).wait_recv()
         acc[...] += rcv[way, j].astype(f32)
 
+    def grads_of_roots(n, carry):
+        foreign, late = n // 2, n & 1
+
+        @pl.when((foreign == 0) | arrives(late))
+        def _():
+            grad_item(chunk_of(foreign, late, z))
+            held[n] = acc[...]
+
+        return carry
+
     def scatter_step(back, carry):
         step = LAST_STEP - back
+
+        @pl.when(step == 1)
+        def _():
+            lax.fori_loop(0, 4, grads_of_roots, 0)
+
         grads_across(step - 1)
 
-        def item(n, carry):
+        def item(i, carry):
+            n = (i + 4) & 7
             foreign, late, way = n // 4, (n // 2) & 1, n & 1
             j = chunk_of(foreign, late, root_of(way, step))
 
@@ -484,7 +493,7 @@
 
         @pl.when(arrives(late))
         def _():
-            grad_item(j)
+            acc[...] = held[2 + late]
             collect(1, late, j)
             snd[j] = acc[...].astype(bf16)
             rs_copy(j, 2, across).start()
@@ -492,13 +501,6 @@
         return carry
 
     lax.fori_loop(0, 2, foreign_root, 0)
-
-    def own_root(late, carry):
-        grad_item(chunk_of(0, late, z))
-        own[late] = acc[...]
-        return carry
-
-    lax.fori_loop(0, 2, own_root, 0)
 
     def tn(a, b):
         return lax.dot_general(a, b, (((0,), (0,)), ((), ())), preferred_element_type=f32)
@@ -525,10 +527,7 @@
         dqt[1, :, cols] = tn(keys, ds_v[NCTX : NCTX + 17, :, cols].reshape(17 * CH, 2 * DH))
     for half, (rows, own_chunk) in enumerate(halves):
         for col in range(0, HC, DH):
-            dq_v[rows, col : col + DH] = (dqt[half, :, col : col + DH].T * SCALE).astype(bf16)
-    dq_store = pltpu.make_async_copy(dq_v, dq_hbm.at[0], out_sem.at[3])
-    dq_store.start()
-
+            dq_out[0, rows, col : col + DH] = (dqt[half, :, col : col + DH].T * SCALE).astype(bf16)
     for late in (0, 1):
         j = chunk_of(0, late, z)
 
@@ -578,7 +577,7 @@
     lax.fori_loop(1, LAST_STEP + 1, sent_step, 0)
 
     def own_total(late, carry):
-        acc[...] = own[late]
+        acc[...] = held[late]
         j = chunk_of(0, late, z)
         collect(0, late, j)
 
@@ -587,32 +586,19 @@
             add_term(2, j, across)
 
         rows = pl.ds(pl.multiple_of(late * CH, CH), CH)
-        dkv_v[0, rows] = (acc[0] * SCALE).astype(bf16)
-        dkv_v[1, rows] = acc[1].astype(bf16)
+        dk_out[0, rows] = (acc[0] * SCALE).astype(bf16)
+        dv_out[0, rows] = acc[1].astype(bf16)
         return carry
 
     lax.fori_loop(0, 2, own_total, 0)
-    kv_stores = [
-        pltpu.make_async_copy(dkv_v.at[n], dst.at[0], out_sem.at[4 + n]) for n, dst in enumerate((dk_hbm, dv_hbm))
-    ]
-    for copy in kv_stores:
+
+def emit(*refs):
+    ins, outs, sem = refs[:6], refs[6:12], refs[12]
+    copies = [pltpu.make_async_copy(ins[n], outs[n], sem.at[n]) for n in range(6)]
+    for copy in copies:
         copy.start()
-
-    for copy in short_stores + [dq_store] + kv_stores:
+    for copy in copies:
         copy.wait()
-
-
-def emit(*refs):
-    ins, outs, held, in_sem, out_sem = refs[:6], refs[6:12], refs[12:18], refs[18], refs[19]
-    loads = [pltpu.make_async_copy(ins[n], held[n], in_sem.at[n]) for n in range(6)]
-    stores = [pltpu.make_async_copy(held[n], outs[n], out_sem.at[n]) for n in range(6)]
-    for load in loads:
-        load.start()
-    for load, store in zip(loads, stores):
-        load.wait()
-        store.start()
-    for store in stores:
-        store.wait()
 
 
 def body(*args):
@@ -639,7 +625,7 @@
         pltpu.VMEM((2, 1, 2 * DH), jnp.int32),
         pltpu.VMEM((2, DH, HC), f32),
         pltpu.VMEM((2, CH, DH), f32),
-        pltpu.VMEM((2, 2, CH, DH), f32),
+        pltpu.VMEM((4, 2, CH, DH), f32),
         pltpu.VMEM((NCHUNK, 2, CH, DH), bf16),
         pltpu.VMEM((3, NCHUNK, 2, CH, DH), bf16),
         pltpu.VMEM((SLOTS, CH, HC), bf16),
@@ -647,13 +633,7 @@
         pltpu.VMEM((SLOTS, CH, DH), bf16),
         pltpu.VMEM((SLOTS, CH, HC), bf16),
         pltpu.VMEM((SLOTS, CH, HC), bf16),
-        pltpu.VMEM((tok, HC), bf16),
-        pltpu.VMEM((2, tok, DH), bf16),
-        pltpu.VMEM((SLOTS, CH, HC), bf16),
-        pltpu.VMEM((SLOTS, CH, DH), bf16),
-        pltpu.VMEM((SLOTS, CH, DH), bf16),
         dma((12,)),
-        dma((6,)),
         dma((NCHUNK, 3)),
         dma((NCHUNK,)),
         dma((NCHUNK,)),
@@ -661,12 +641,12 @@
     ]
     grads = pl.pallas_call(
         kernel,
-        out_shape=out_shape,
+        out_shape=[pltpu.VMEM(out.shape, out.dtype) for out in out_shape],
         in_specs=in_specs,
-        out_specs=[any_spec] * 6,
+        out_specs=[pl.BlockSpec(memory_space=pltpu.VMEM)] * 6,
         scratch_shapes=scratch,
         compiler_params=pltpu.CompilerParams(
-            collective_id=0, has_side_effects=True, vmem_limit_bytes=60 * 1024 * 1024
+            collective_id=0, has_side_effects=True, vmem_limit_bytes=56 * 1024 * 1024
         ),
         name="attention_backward",
     )(*args)
@@ -674,10 +654,9 @@
         pl.pallas_call(
             emit,
             out_shape=out_shape,
-            in_specs=[any_spec] * 6,
+            in_specs=[pl.BlockSpec(memory_space=pltpu.VMEM)] * 6,
             out_specs=[any_spec] * 6,
-            scratch_shapes=[pltpu.VMEM(out.shape, bf16) for out in out_shape] + [dma((6,)), dma((6,))],
-            compiler_params=pltpu.CompilerParams(vmem_limit_bytes=60 * 1024 * 1024),
+            scratch_shapes=[dma((6,))],
             name="emit",
         )(*grads)
     )

time: 61.6 us -> 64.9 us (1.054)
  local copies, waits for them, and re-layouts: 0 us -> 4.2 us
  Pallas kernels: 59.6 us -> 58.8 us
    unnamed x0 -> x12, local copies, waits for them, and re-layouts: none -> 4.2 us
    pallas_call x2, Pallas kernels: 59.6 us -> 58.8 us  [the longest x1 56.3 us: body(): pl.pallas_call(kernel, out_shape=[pltpu.VMEM(out.shape, out.dtype) for ou...]
where the time goes in v5:
time: 64.9 us; the launch traced here: 64.3 us
  Pallas kernels  58.8 us (91%)
  local copies, waits for them, and re-layouts  4.2 us (6%)
  between operations  1.31 us (2%)
    pallas_call x1, Pallas kernels, body(): pl.pallas_call(kernel, out_shape=[pltpu.VMEM(out.shape, out.dtype) for ou...  56.3 us
    unnamed x12, local copies, waits for them, and re-layouts  4.2 us
    pallas_call x1, Pallas kernels, body(): pl.pallas_call(emit, out_shape=out_shape, in_specs=[pl.BlockSpec(memory_s...  2.54 us

profile of v5, /device:TPU:8, one launch (start us, length us, event | category | flops | bytes accessed | tf_op | source)
XLA Modules:
  0.0 64.3 jit_solution(11603010137550172010)
XLA Ops:
  1.3 56.3 %attention_backward.1 = (bf16[1,256,768]{2,1,0:T(8,128)(2,1)S(1)}, bf16[1,256,128]{2,1,0:T(8,128)(2,1)S(1)}, bf16[1,256,128]{2,1,0:T(8,128)(2,1)S(1)}, bf16[1,4,...) custom-call(bf16[1,256,768]{2,1,0:T(8,128)(2,1)} %q_hbm.1, ...), custom_call_target="tpu_custom_call" | custom-call | tf_op jit(solution)/shard_map/attention_backward/pallas_call | solution.py:642
  57.6 0.0 copy-start
  57.6 0.9 %copy-done = bf16[1,4,128,768]{3,2,1,0:T(8,128)(2,1)} copy-done((bf16[1,4,128,768]{3,2,1,0:T(8,128)(2,1)}, bf16[1,4,128,768]{3,2,1,0:T(8,128)(2,1)S(1)}, u32[]{:S(2)}) %copy-start) | copy-done | bytes 786456
  58.5 0.0 copy-start.1
  58.5 0.8 %copy-done.1 = bf16[1,256,768]{2,1,0:T(8,128)(2,1)} copy-done((bf16[1,256,768]{2,1,0:T(8,128)(2,1)}, bf16[1,256,768]{2,1,0:T(8,128)(2,1)S(1)}, u32[]{:S(2)}) %copy-start.1) | copy-done | bytes 393240
  59.2 0.0 copy-start.2
  59.2 0.6 %copy-done.2 = bf16[1,4,128,128]{3,2,1,0:T(8,128)(2,1)} copy-done((bf16[1,4,128,128]{3,2,1,0:T(8,128)(2,1)}, bf16[1,4,128,128]{3,2,1,0:T(8,128)(2,1)S(1)}, u32[]{:S(2)}) %copy-start.2) | copy-done | bytes 131096
  59.9 0.0 copy-start.3
  59.9 0.7 %copy-done.3 = bf16[1,4,128,128]{3,2,1,0:T(8,128)(2,1)} copy-done((bf16[1,4,128,128]{3,2,1,0:T(8,128)(2,1)}, bf16[1,4,128,128]{3,2,1,0:T(8,128)(2,1)S(1)}, u32[]{:S(2)}) %copy-start.3) | copy-done | bytes 131096
  60.5 0.0 copy-start.4
  60.5 0.6 copy-done.4
  61.2 0.0 copy-start.5
  61.2 0.6 copy-done.5
  61.8 2.5 %emit.1 = (bf16[1,256,768]{2,1,0:T(8,128)(2,1)}, bf16[1,256,128]{2,1,0:T(8,128)(2,1)}, bf16[1,256,128]{2,1,0:T(8,128)(2,1)}, bf16[1,4,128,768]{3,2,1,0:T(8,128)(...) custom-call(bf16[1,256,768]{2,1,0:T(8,128)(2,1)} %copy-done.1, bf16[1,256,128]{2,1,0:T(8,128)(2,1)} %copy-done.4, ...), custom_call_target="tpu_custom_call" | custom-call | tf_op jit(solution)/shard_map/emit/pallas_call | solution.py:654
Async XLA Ops:
  57.6 0.9 %copy-start = (bf16[1,4,128,768]{3,2,1,0:T(8,128)(2,1)}, bf16[1,4,128,768]{3,2,1,0:T(8,128)(2,1)S(1)}, u32[]{:S(2)}) copy-start(bf16[1,4,128,768]{3,2,1,0:T(8,128)(2,1)S(1)} %get-tuple-element.15.refs_3_) | copy-start | bytes 2359300
  58.5 0.8 %copy-start.1 = (bf16[1,256,768]{2,1,0:T(8,128)(2,1)}, bf16[1,256,768]{2,1,0:T(8,128)(2,1)S(1)}, u32[]{:S(2)}) copy-start(bf16[1,256,768]{2,1,0:T(8,128)(2,1)S(1)} %get-tuple-element.12.refs_0_) | copy-start | bytes 1179652
  59.2 0.7 %copy-start.2 = (bf16[1,4,128,128]{3,2,1,0:T(8,128)(2,1)}, bf16[1,4,128,128]{3,2,1,0:T(8,128)(2,1)S(1)}, u32[]{:S(2)}) copy-start(bf16[1,4,128,128]{3,2,1,0:T(8,128)(2,1)S(1)} %get-tuple-element.16.refs_4_) | copy-start | bytes 393220
  59.9 0.7 %copy-start.3 = (bf16[1,4,128,128]{3,2,1,0:T(8,128)(2,1)}, bf16[1,4,128,128]{3,2,1,0:T(8,128)(2,1)S(1)}, u32[]{:S(2)}) copy-start(bf16[1,4,128,128]{3,2,1,0:T(8,128)(2,1)S(1)} %get-tuple-element.17.refs_5_) | copy-start | bytes 393220
  60.5 0.6 copy-start.4
  61.2 0.6 copy-start.5

commit v6 on v4

--- a/solution.py
+++ b/solution.py
@@ -23,23 +23,23 @@
 LAST_STEP = 4
 
 HOPS_UP = {
-    (0, 0, 0): (3, 3, 3, 4, 3, 2, 1, 0),
-    (0, 0, 1): (0, 0, 0, 0, 0, 4, 4, 4),
-    (0, 1, 0): (0, 0, 3, 4, 3, 2, 4, 4),
-    (0, 1, 1): (4, 3, 4, 3, 4, 3, 4, 3),
-    (1, 0, 0): (4, 4, 4, 4, 4, 4, 4, 4),
+    (0, 0, 0): (4, 4, 3, 4, 3, 2, 1, 0),
+    (0, 0, 1): (0, 0, 0, 0, 0, 3, 4, 4),
+    (0, 1, 0): (0, 0, 0, 4, 0, 0, 1, 4),
+    (0, 1, 1): (4, 3, 4, 4, 3, 4, 0, 4),
+    (1, 0, 0): (4, 3, 4, 4, 3, 4, 4, 4),
     (1, 0, 1): (0, 0, 0, 0, 0, 4, 4, 4),
-    (1, 1, 0): (4, 3, 4, 3, 4, 3, 4, 3),
+    (1, 1, 0): (4, 2, 3, 4, 4, 3, 3, 4),
     (1, 1, 1): (0, 0, 0, 0, 0, 0, 0, 0),
 }
 HOPS_DOWN = {
-    (0, 0, 0): (4, 4, 4, 0, 0, 0, 0, 0),
-    (0, 0, 1): (0, 1, 2, 3, 4, 3, 3, 3),
-    (0, 1, 0): (1, 3, 4, 0, 1, 3, 3, 3),
-    (0, 1, 1): (3, 4, 3, 4, 3, 4, 3, 4),
-    (1, 0, 0): (3, 3, 3, 3, 3, 3, 3, 3),
+    (0, 0, 0): (3, 3, 4, 3, 0, 0, 0, 0),
+    (0, 0, 1): (0, 1, 2, 3, 4, 4, 3, 3),
+    (0, 1, 0): (0, 0, 4, 0, 0, 0, 4, 0),
+    (0, 1, 1): (3, 4, 3, 2, 4, 3, 4, 3),
+    (1, 0, 0): (3, 4, 3, 3, 4, 3, 3, 3),
     (1, 0, 1): (0, 1, 2, 3, 4, 3, 3, 3),
-    (1, 1, 0): (3, 4, 3, 4, 3, 4, 3, 4),
+    (1, 1, 0): (3, 4, 4, 2, 3, 4, 4, 3),
     (1, 1, 1): (0, 0, 0, 0, 0, 0, 0, 0),
 }
 
@@ -111,7 +111,7 @@
     q_hbm, k_hbm, v_hbm, o_hbm, do_hbm, doc_ref,
     qs_hbm, ks_hbm, vs_hbm, os_hbm, dos_hbm, slen_ref, scount_ref,
     dq_hbm, dk_hbm, dv_hbm, dqs_hbm, dks_hbm, dvs_hbm,
-    kv, q_v, o_v, do_v, qt_v, dot_v, scores, ds_v, m_v, l_v, lse_v, delta_v, lo_v, dqt, acc, own,
+    kv, q_v, o_v, do_v, qt_v, dot_v, scores, ds_v, m_v, l_v, lse_v, delta_v, lo_v, dqt, acc, held,
     snd, rcv, qs_v, ks_v, vs_v, os_v, dos_v, dq_v, dkv_v, dqs_v, dks_v, dvs_v,
     in_sem, out_sem, ag_send, ag_recv, rs_send, rs_recv,
 ):
@@ -353,32 +353,34 @@
             lax.fori_loop(0, 4, item, 0)
 
     def gather_step(step, carry):
-        for n in range(8):
-            foreign, late, way = n // 4, n // 2 % 2, n % 2
-            j = chunk_of(foreign, late, root_of(way, step))
-
-            @pl.when(has(step, n))
-            def _():
-                ag_copy(j, way, beside[way]).wait_recv()
-
-            @pl.when(forwards(step, n))
-            def _():
-                ag_copy(j, way, beside[way]).start()
-
-            if foreign == 0:
-
-                @pl.when(goes_across(step, n))
+        def pair(q, carry):
+            foreign, late = q // 2, q & 1
+            for way in (0, 1):
+                j = chunk_of(foreign, late, root_of(way, step))
+
+                @pl.when(has(step, 2 * q + way))
+                def _():
+                    ag_copy(j, way, beside[way]).wait_recv()
+
+                @pl.when(forwards(step, 2 * q + way))
+                def _():
+                    ag_copy(j, way, beside[way]).start()
+
+                @pl.when((foreign == 0) & goes_across(step, (2 * q + way) & 3))
                 def _():
                     ag_copy(j, 2, across).start()
 
-        short_slot(step - 1)
-
-        def item(n, carry):
-            foreign, late, way = n // 4, (n // 2) & 1, n & 1
-            score_item(chunk_of(foreign, late, root_of(way, step)), has(step, n))
-            return carry
-
-        lax.fori_loop(0, 8, item, carry)
+            @pl.when(q == 0)
+            def _():
+                short_slot(step - 1)
+
+            def item(way, carry):
+                score_item(chunk_of(foreign, late, root_of(way, step)), has(step, 2 * q + way))
+                return carry
+
+            return lax.fori_loop(0, 2, item, carry)
+
+        lax.fori_loop(0, 4, pair, carry)
         score_across(step - 1)
         return carry
 
@@ -442,11 +444,27 @@
         rs_copy(j, way, target).wait_recv()
         acc[...] += rcv[way, j].astype(f32)
 
+    def grads_of_roots(n, carry):
+        foreign, late = n // 2, n & 1
+
+        @pl.when((foreign == 0) | arrives(late))
+        def _():
+            grad_item(chunk_of(foreign, late, z))
+            held[n] = acc[...]
+
+        return carry
+
     def scatter_step(back, carry):
         step = LAST_STEP - back
+
+        @pl.when(step == 1)
+        def _():
+            lax.fori_loop(0, 4, grads_of_roots, 0)
+
         grads_across(step - 1)
 
-        def item(n, carry):
+        def item(i, carry):
+            n = (i + 4) & 7
             foreign, late, way = n // 4, (n // 2) & 1, n & 1
             j = chunk_of(foreign, late, root_of(way, step))
 
@@ -484,7 +502,7 @@
 
         @pl.when(arrives(late))
         def _():
-            grad_item(j)
+            acc[...] = held[2 + late]
             collect(1, late, j)
             snd[j] = acc[...].astype(bf16)
             rs_copy(j, 2, across).start()
@@ -492,13 +510,6 @@
         return carry
 
     lax.fori_loop(0, 2, foreign_root, 0)
-
-    def own_root(late, carry):
-        grad_item(chunk_of(0, late, z))
-        own[late] = acc[...]
-        return carry
-
-    lax.fori_loop(0, 2, own_root, 0)
 
     def tn(a, b):
         return lax.dot_general(a, b, (((0,), (0,)), ((), ())), preferred_element_type=f32)
@@ -578,7 +589,7 @@
     lax.fori_loop(1, LAST_STEP + 1, sent_step, 0)
 
     def own_total(late, carry):
-        acc[...] = own[late]
+        acc[...] = held[late]
         j = chunk_of(0, late, z)
         collect(0, late, j)
 
@@ -604,8 +615,17 @@
 
 def emit(*refs):
     ins, outs, held, in_sem, out_sem = refs[:6], refs[6:12], refs[12:18], refs[18], refs[19]
-    loads = [pltpu.make_async_copy(ins[n], held[n], in_sem.at[n]) for n in range(6)]
-    stores = [pltpu.make_async_copy(held[n], outs[n], out_sem.at[n]) for n in range(6)]
+    pieces = [(n, pl.ds(0, 1), pl.ds(half * CH, CH)) for n in (0, 1, 2) for half in (0, 1)]
+    pieces += [(3, pl.ds(0, 1), pl.ds(slot, 1)) for slot in range(SLOTS)]
+    pieces += [(n, pl.ds(0, 1), pl.ds(0, SLOTS)) for n in (4, 5)]
+    loads = [
+        pltpu.make_async_copy(ins[n].at[one, part], held[n].at[one, part], in_sem.at[i])
+        for i, (n, one, part) in enumerate(pieces)
+    ]
+    stores = [
+        pltpu.make_async_copy(held[n].at[one, part], outs[n].at[one, part], out_sem.at[i])
+        for i, (n, one, part) in enumerate(pieces)
+    ]
     for load in loads:
         load.start()
     for load, store in zip(loads, stores):
@@ -639,7 +659,7 @@
         pltpu.VMEM((2, 1, 2 * DH), jnp.int32),
         pltpu.VMEM((2, DH, HC), f32),
         pltpu.VMEM((2, CH, DH), f32),
-        pltpu.VMEM((2, 2, CH, DH), f32),
+        pltpu.VMEM((4, 2, CH, DH), f32),
         pltpu.VMEM((NCHUNK, 2, CH, DH), bf16),
         pltpu.VMEM((3, NCHUNK, 2, CH, DH), bf16),
         pltpu.VMEM((SLOTS, CH, HC), bf16),
@@ -676,7 +696,7 @@
             out_shape=out_shape,
             in_specs=[any_spec] * 6,
             out_specs=[any_spec] * 6,
-            scratch_shapes=[pltpu.VMEM(out.shape, bf16) for out in out_shape] + [dma((6,)), dma((6,))],
+            scratch_shapes=[pltpu.VMEM(out.shape, bf16) for out in out_shape] + [dma((12,)), dma((12,))],
             compiler_params=pltpu.CompilerParams(vmem_limit_bytes=60 * 1024 * 1024),
             name="emit",
         )(*grads)

time: 61.6 us -> 57.9 us (0.940)
  Pallas kernels: 59.6 us -> 56.1 us
    pallas_call x1, Pallas kernels: 57.2 us -> 53.7 us  [body(): pl.pallas_call(kernel, out_shape=out_shape, in_specs=in_specs, out_specs=...]
where the time goes in v6:
time: 57.9 us; the launch traced here: 57.4 us
  Pallas kernels  56.1 us (97%)
  between operations  1.29 us (2%)
    pallas_call x1, Pallas kernels, body(): pl.pallas_call(kernel, out_shape=out_shape, in_specs=in_specs, out_specs=...  53.7 us
    pallas_call x1, Pallas kernels, body(): pl.pallas_call(emit, out_shape=out_shape, in_specs=[any_spec] * 6, out_sp...  2.36 us

profile of v6, /device:TPU:8, one launch (start us, length us, event | category | flops | bytes accessed | tf_op | source)
XLA Modules:
  0.0 57.4 jit_solution(3279593513126507077)
XLA Ops:
  1.3 53.7 %attention_backward.1 = (bf16[1,256,768]{2,1,0:T(8,128)(2,1)}, bf16[1,256,128]{2,1,0:T(8,128)(2,1)}, bf16[1,256,128]{2,1,0:T(8,128)(2,1)}, bf16[1,4,128,768]{3,2...) custom-call(bf16[1,256,768]{2,1,0:T(8,128)(2,1)} %q_hbm.1, ...), custom_call_target="tpu_custom_call" | custom-call | tf_op jit(solution)/shard_map/attention_backward/pallas_call | solution.py:682
  55.0 2.4 %emit.1 = (bf16[1,256,768]{2,1,0:T(8,128)(2,1)}, bf16[1,256,128]{2,1,0:T(8,128)(2,1)}, bf16[1,256,128]{2,1,0:T(8,128)(2,1)}, bf16[1,4,128,768]{3,2,1,0:T(8,128)(...) custom-call(bf16[1,256,768]{2,1,0:T(8,128)(2,1)} %get-tuple-element.12.refs_0_, ...), custom_call_target="tpu_custom_call" | custom-call | tf_op jit(solution)/shard_map/emit/pallas_call | solution.py:694

commit v7 on v6

--- a/solution.py
+++ b/solution.py
@@ -22,36 +22,60 @@
 NEG = -1e30
 LAST_STEP = 4
 
-HOPS_UP = {
-    (0, 0, 0): (4, 4, 3, 4, 3, 2, 1, 0),
-    (0, 0, 1): (0, 0, 0, 0, 0, 3, 4, 4),
-    (0, 1, 0): (0, 0, 0, 4, 0, 0, 1, 4),
-    (0, 1, 1): (4, 3, 4, 4, 3, 4, 0, 4),
-    (1, 0, 0): (4, 3, 4, 4, 3, 4, 4, 4),
-    (1, 0, 1): (0, 0, 0, 0, 0, 4, 4, 4),
-    (1, 1, 0): (4, 2, 3, 4, 4, 3, 3, 4),
-    (1, 1, 1): (0, 0, 0, 0, 0, 0, 0, 0),
-}
-HOPS_DOWN = {
-    (0, 0, 0): (3, 3, 4, 3, 0, 0, 0, 0),
-    (0, 0, 1): (0, 1, 2, 3, 4, 4, 3, 3),
-    (0, 1, 0): (0, 0, 4, 0, 0, 0, 4, 0),
-    (0, 1, 1): (3, 4, 3, 2, 4, 3, 4, 3),
-    (1, 0, 0): (3, 4, 3, 3, 4, 3, 3, 3),
-    (1, 0, 1): (0, 1, 2, 3, 4, 3, 3, 3),
-    (1, 1, 0): (3, 4, 4, 2, 3, 4, 4, 3),
-    (1, 1, 1): (0, 0, 0, 0, 0, 0, 0, 0),
-}
+HOPS_UP = (
+    {
+        (0, 0, 0): (4, 3, 4, 3, 3, 2, 1, 0),
+        (0, 0, 1): (0, 0, 0, 0, 0, 3, 3, 4),
+        (0, 1, 0): (0, 0, 4, 3, 0, 0, 0, 3),
+        (0, 1, 1): (3, 3, 0, 4, 4, 3, 4, 4),
+        (1, 0, 0): (3, 3, 3, 4, 4, 4, 3, 3),
+        (1, 0, 1): (0, 0, 3, 0, 0, 4, 4, 4),
+        (1, 1, 0): (2, 1, 3, 4, 4, 3, 3, 3),
+        (1, 1, 1): (0, 0, 0, 0, 0, 0, 0, 0),
+    },
+    {
+        (0, 0, 0): (4, 3, 3, 4, 3, 2, 1, 0),
+        (0, 0, 1): (0, 0, 0, 0, 0, 3, 4, 4),
+        (0, 1, 0): (0, 0, 4, 3, 0, 0, 0, 4),
+        (0, 1, 1): (4, 3, 1, 4, 4, 3, 4, 2),
+        (1, 0, 0): (4, 3, 4, 3, 4, 4, 3, 3),
+        (1, 0, 1): (0, 0, 3, 0, 0, 4, 3, 4),
+        (1, 1, 0): (1, 4, 3, 0, 4, 3, 4, 3),
+        (1, 1, 1): (0, 0, 0, 0, 0, 0, 0, 0),
+    },
+)
+HOPS_DOWN = (
+    {
+        (0, 0, 0): (3, 4, 3, 4, 3, 0, 0, 0),
+        (0, 0, 1): (0, 1, 2, 3, 4, 4, 4, 3),
+        (0, 1, 0): (0, 0, 3, 4, 0, 3, 4, 4),
+        (0, 1, 1): (4, 4, 4, 1, 1, 4, 0, 3),
+        (1, 0, 0): (4, 4, 4, 3, 3, 3, 4, 4),
+        (1, 0, 1): (0, 1, 2, 3, 4, 3, 3, 3),
+        (1, 1, 0): (4, 4, 4, 2, 2, 4, 4, 4),
+        (1, 1, 1): (0, 0, 0, 0, 0, 0, 0, 0),
+    },
+    {
+        (0, 0, 0): (3, 4, 4, 0, 0, 0, 0, 0),
+        (0, 0, 1): (0, 1, 2, 3, 4, 4, 3, 3),
+        (0, 1, 0): (1, 0, 0, 4, 0, 1, 4, 3),
+        (0, 1, 1): (2, 4, 4, 0, 1, 4, 1, 4),
+        (1, 0, 0): (3, 4, 3, 4, 3, 3, 4, 4),
+        (1, 0, 1): (3, 1, 2, 3, 4, 3, 4, 3),
+        (1, 1, 0): (4, 3, 4, 4, 3, 4, 3, 4),
+        (1, 1, 1): (0, 0, 0, 0, 0, 0, 0, 0),
+    },
+)
 
 
 def needed(j, c):
     return j <= c or 15 - c <= j <= 31 - c
 
 
-def device_masks(c):
+def device_masks(c, core):
     x, z = divmod(c, NZ)
     across = (1 - x) * NZ + z
-    hops = (HOPS_UP, HOPS_DOWN)
+    hops = (HOPS_UP[core], HOPS_DOWN[core])
 
     def chunk(plane, late, zr):
         owner = plane * NZ + zr
@@ -125,10 +149,12 @@
     across = (1 - x) * NZ + z
     beside = (x * NZ + z_up, x * NZ + z_down)
 
-    masks = [jnp.int32(m) for m in device_masks(0)]
-    for device in range(1, NCTX):
-        here = c == device
-        masks = [jnp.where(here, jnp.int32(m), old) for m, old in zip(device_masks(device), masks)]
+    core = lax.axis_index("dp") & 1
+    masks = [jnp.int32(m) for m in device_masks(0, 0)]
+    for device in range(1, 2 * NCTX):
+        here = c + core * NCTX == device
+        values = device_masks(device % NCTX, device // NCTX)
+        masks = [jnp.where(here, jnp.int32(m), old) for m, old in zip(values, masks)]
     has_mask, forward_mask, over_mask, root_mask = masks
 
     def bit(mask, n):
@@ -200,14 +226,13 @@
             ((qs_hbm, qs_v), (ks_hbm, ks_v), (vs_hbm, vs_v), (os_hbm, os_v), (dos_hbm, dos_v))
         )
     ]
-    for copy in kv_loads + long_loads + short_loads:
-        copy.start()
-
     barrier = pltpu.get_barrier_semaphore()
     for target in beside + (across,):
         pl.semaphore_signal(
             barrier, inc=1, device_id={"ctx": target}, device_id_type=pl.DeviceIdType.MESH
         )
+    for copy in kv_loads:
+        copy.start()
     pl.semaphore_wait(barrier, 3)
 
     for copy in kv_loads:
@@ -227,6 +252,8 @@
             def _():
                 ag_copy(j, way, beside[way]).start()
 
+    for copy in long_loads + short_loads:
+        copy.start()
     for copy in long_loads:
         copy.wait()
     halves = [(pl.ds(half * CH, CH), own_chunk) for half, own_chunk in ((0, c), (1, late_own))]

time: 57.9 us -> 57.9 us (level)
  no operation moved by 1% of the time
where the time goes in v7:
time: 57.9 us; the launch traced here: 57.8 us
  Pallas kernels  56.5 us (98%)
  between operations  1.29 us (2%)
    pallas_call x1, Pallas kernels, body(): pl.pallas_call(kernel, out_shape=out_shape, in_specs=in_specs, out_specs=...  54.1 us
    pallas_call x1, Pallas kernels, body(): pl.pallas_call(emit, out_shape=out_shape, in_specs=[any_spec] * 6, out_sp...  2.36 us

profile of v7, /device:TPU:8, one launch (start us, length us, event | category | flops | bytes accessed | tf_op | source)
XLA Modules:
  0.0 57.8 jit_solution(3891478372371374834)
XLA Ops:
  1.3 54.1 %attention_backward.1 = (bf16[1,256,768]{2,1,0:T(8,128)(2,1)}, bf16[1,256,128]{2,1,0:T(8,128)(2,1)}, bf16[1,256,128]{2,1,0:T(8,128)(2,1)}, bf16[1,4,128,768]{3,2...) custom-call(bf16[1,256,768]{2,1,0:T(8,128)(2,1)} %q_hbm.1, ...), custom_call_target="tpu_custom_call" | custom-call | tf_op jit(solution)/shard_map/attention_backward/pallas_call | solution.py:709
  55.4 2.4 %emit.1 = (bf16[1,256,768]{2,1,0:T(8,128)(2,1)}, bf16[1,256,128]{2,1,0:T(8,128)(2,1)}, bf16[1,256,128]{2,1,0:T(8,128)(2,1)}, bf16[1,4,128,768]{3,2,1,0:T(8,128)(...) custom-call(bf16[1,256,768]{2,1,0:T(8,128)(2,1)} %get-tuple-element.12.refs_0_, ...), custom_call_target="tpu_custom_call" | custom-call | tf_op jit(solution)/shard_map/emit/pallas_call | solution.py:721
